TPU v7x, 32 devices: a whole 2x2x4 slice. The times are simulated.
32 devices in a mesh: head: 4 (over y, x), batch: 8 (over z, core).
Axes of the slice: x: 2, y: 2, z: 4, core: 2. Of those that a mesh axis runs over, the one named last changes fastest.
Arguments:
- tokens: bfloat16 [384, 196, 256], P('batch'), may hold values from -6 to 6
- image_count: int32 [8], P('batch'), may hold values from 16 to 48, as said below
- token_place: int32 [196], replicated, may hold values from 0 to 195, each once
- qkv_weight: float32 [4, 128, 256], P('head'), may hold values from -0.375 to 0.375
- bias_table: float32 [4, 196], P('head'), may hold values from -4 to 4
- proj_weight: float32 [256, 256], replicated, may hold values from -0.375 to 0.375
- attention_gain: float32 [256], replicated, may hold values from 0.5 to 1.5
- attention_shift: float32 [256], replicated, may hold values from -3 to 3
- up_weight: float32 [256, 512], P(None, 'head'), may hold values from -0.375 to 0.375
- hidden_gain: float32 [512], P('head'), may hold values from 0.5 to 1.5
- hidden_shift: float32 [512], P('head'), may hold values from -3 to 3
- down_weight: float32 [512, 256], P('head'), may hold values from -0.25 to 0.25
- output_gain: float32 [256], replicated, may hold values from 0.5 to 1.5
- output_shift: float32 [256], replicated, may hold values from -3 to 3
- cotangent: bfloat16 [384, 196, 256], P('batch', 'head'), may hold values from -6 to 6
Outputs:
- output: float32 [384, 196, 256], P('batch', 'head')
- tokens_grad: float32 [384, 196, 256], P('batch', 'head')
- qkv_grad: float32 [4, 128, 256], P('head')
- bias_grad: float32 [4, 196], P('head')
- proj_grad: float32 [256, 256], P('head')
- attention_gain_grad: float32 [256], replicated
- attention_shift_grad: float32 [256], replicated
- up_grad: float32 [256, 512], P(None, 'head')
- hidden_gain_grad: float32 [512], P('head')
- hidden_shift_grad: float32 [512], P('head')
- down_grad: float32 [512, 256], P('head')
- output_gain_grad: float32 [256], replicated
- output_shift_grad: float32 [256], replicated
Inputs may be any that keep to these rules, and one draw needn't show every extreme that they name: Index b of batch holds image_count[b] real images in its first slots of 48; the other slots are padding that no statistic reads.
All inputs are finite; a program needn't handle non-finite values.
Results may differ from a plain program's by a relative error of at most 0.019.
The roundings to bfloat16 on the way count: a program that leaves them out, or rounds other values in their place, can miss the bound.
Values may be sent and summed in bfloat16 or wider, within the bound.
A program may use at most 192 MiB of HBM per device.

v0:
```python
import jax
import jax.numpy as jnp
from jax import lax
from jax.sharding import PartitionSpec as P

KEY = 32
VAL = 64
SIDE = 14
OFFS = 196


epsilon = 1e-05
group_images = 4


def silu(value):
    return value * jax.nn.sigmoid(value)


def silu_slope(value):
    sigmoid_value = jax.nn.sigmoid(value)
    return sigmoid_value * (1.0 + value * (1.0 - sigmoid_value))


def on_device(
    tokens,
    image_count,
    token_place,
    qkv_weight,
    bias_table,
    proj_weight,
    attention_gain,
    attention_shift,
    up_weight,
    hidden_gain,
    hidden_shift,
    down_weight,
    output_gain,
    output_shift,
    cotangent,
):
    images, length, width = tokens.shape
    heads_here = qkv_weight.shape[0]
    hidden_here = up_weight.shape[1]
    token_share = cotangent.shape[1]
    head_slot = lax.axis_index("head")
    token_start = head_slot * token_share
    groups = images // group_images
    valid = (jnp.arange(images, dtype=jnp.int32) < image_count[0]).astype(jnp.float32)
    rows_valid = valid[:, None, None]
    scaling = KEY ** (-0.5)
    grid_rows = token_place // SIDE
    grid_cols = token_place % SIDE
    offset_index = jnp.abs(grid_rows[:, None] - grid_rows[None, :]) * SIDE + jnp.abs(
        grid_cols[:, None] - grid_cols[None, :]
    )
    onehot = (offset_index[:, :, None] == jnp.arange(OFFS, dtype=jnp.int32)[None, None, :]).astype(
        jnp.float32
    )
    position_bias = jnp.einsum("hk,tsk->hts", bias_table, onehot, precision=lax.Precision.HIGHEST)
    qkv_low = qkv_weight.astype(jnp.bfloat16)
    proj_low = proj_weight.astype(jnp.bfloat16)
    token_groups = tokens.reshape(groups, group_images, length, width)

    def scores_of(mixed):
        return (
            jnp.einsum(
                "ithc,ishc->ihts",
                mixed[..., :KEY],
                mixed[..., KEY : 2 * KEY],
                preferred_element_type=jnp.float32,
            )
            * scaling
            + position_bias[None]
        )

    def attend(block):
        mixed = jnp.einsum(
            "itd,hcd->ithc", block, qkv_low, preferred_element_type=jnp.float32
        ).astype(jnp.bfloat16)
        scores = scores_of(mixed)
        highest_score = jnp.max(scores, axis=-1, keepdims=True)
        raised = jnp.exp(scores - highest_score)
        total = jnp.sum(raised, axis=-1, keepdims=True)
        weights = (raised / total).astype(jnp.bfloat16)
        attended = jnp.einsum(
            "ihts,ishc->ithc", weights, mixed[..., 2 * KEY :], preferred_element_type=jnp.float32
        )
        return (mixed, attended, highest_score + jnp.log(total))

    mixed_all, attended_all, log_total = lax.map(attend, token_groups)
    active = silu(attended_all).astype(jnp.bfloat16).reshape(images, length, heads_here * VAL)

    def normalize(values, first_sum, second_sum, count):
        mean = first_sum / count
        inverse = lax.rsqrt(second_sum / count - mean * mean + epsilon)
        return ((values - mean) * inverse, inverse)

    def unnormalize(grad, normed, inverse, gain, shift_sum, gain_sum, mask, count):
        return mask * gain * inverse * (grad - shift_sum / count - normed * gain_sum / count)

    up_low = up_weight.astype(jnp.bfloat16)
    down_low = down_weight.astype(jnp.bfloat16)
    projected = jnp.einsum(
        "itc,cd->itd",
        lax.all_gather(active, "head", axis=2, tiled=True),
        proj_low,
        preferred_element_type=jnp.float32,
    )
    first, second, seen = lax.psum(
        (
            jnp.sum(projected * rows_valid, axis=(0, 1)),
            jnp.sum(projected * projected * rows_valid, axis=(0, 1)),
            jnp.sum(valid)[None] * length,
        ),
        "batch",
    )
    normed_one, inverse_one = normalize(projected, first, second, seen)
    residual = tokens.astype(jnp.float32) + attention_gain * normed_one + attention_shift
    residual_low = residual.astype(jnp.bfloat16)
    hidden = jnp.einsum("itd,df->itf", residual_low, up_low, preferred_element_type=jnp.float32)
    first, second = lax.psum(
        (
            jnp.sum(hidden * rows_valid, axis=(0, 1)),
            jnp.sum(hidden * hidden * rows_valid, axis=(0, 1)),
        ),
        "batch",
    )
    normed_two, inverse_two = normalize(hidden, first, second, seen)
    shaped = hidden_gain * normed_two + hidden_shift
    active_two = silu(shaped).astype(jnp.bfloat16)
    partial_out = jnp.einsum(
        "itf,fd->itd", active_two, down_low, preferred_element_type=jnp.float32
    )
    outgoing = lax.psum_scatter(
        partial_out.astype(jnp.bfloat16), "head", scatter_dimension=1, tiled=True
    ).astype(jnp.float32)
    residual_own = lax.dynamic_slice_in_dim(residual, token_start, token_share, 1)
    first, second = lax.psum(
        (
            jnp.sum(outgoing * rows_valid, axis=(0, 1)),
            jnp.sum(outgoing * outgoing * rows_valid, axis=(0, 1)),
        ),
        ("head", "batch"),
    )
    normed_three, inverse_three = normalize(outgoing, first, second, seen)
    output = rows_valid * (residual_own + output_gain * normed_three + output_shift)
    upstream = cotangent.astype(jnp.float32) * rows_valid
    shift_three, gain_three = lax.psum(
        (jnp.sum(upstream, axis=(0, 1)), jnp.sum(upstream * normed_three, axis=(0, 1))),
        ("head", "batch"),
    )
    grad_outgoing = unnormalize(
        upstream,
        normed_three,
        inverse_three,
        output_gain,
        shift_three,
        gain_three,
        rows_valid,
        seen,
    ).astype(jnp.bfloat16)
    piece = lax.all_gather(grad_outgoing, "head", axis=1, tiled=True)
    grad_act = jnp.zeros((images, length, hidden_here), jnp.float32)
    part = jnp.einsum("itd,fd->itf", piece, down_low, preferred_element_type=jnp.float32)
    grad_act = part
    act_rows = active_two
    weight_grad = jnp.einsum("itf,itd->fd", act_rows, piece, preferred_element_type=jnp.float32)
    grad_active_two = grad_act
    down_grad = weight_grad
    grad_shaped = grad_active_two * silu_slope(shaped)
    shift_two, gain_two = lax.psum(
        (jnp.sum(grad_shaped, axis=(0, 1)), jnp.sum(grad_shaped * normed_two, axis=(0, 1))), "batch"
    )
    grad_hidden = unnormalize(
        grad_shaped, normed_two, inverse_two, hidden_gain, shift_two, gain_two, rows_valid, seen
    ).astype(jnp.bfloat16)
    up_grad = jnp.einsum(
        "itd,itf->df", residual_low, grad_hidden, preferred_element_type=jnp.float32
    )
    grad_residual = jnp.einsum(
        "itf,df->itd", grad_hidden, up_low, preferred_element_type=jnp.float32
    )
    grad_residual = lax.dynamic_update_slice_in_dim(
        grad_residual,
        lax.dynamic_slice_in_dim(grad_residual, token_start, token_share, 1) + upstream,
        token_start,
        1,
    )
    own_rows = lax.dynamic_slice_in_dim(proj_low, head_slot * heads_here * VAL, heads_here * VAL, 0)
    grad_view = lax.psum(grad_residual.astype(jnp.bfloat16), "head").astype(jnp.float32)
    shift_one, gain_one = lax.psum(
        (jnp.sum(grad_view, axis=(0, 1)), jnp.sum(grad_view * normed_one, axis=(0, 1))), "batch"
    )
    grad_projected = unnormalize(
        grad_view, normed_one, inverse_one, attention_gain, shift_one, gain_one, rows_valid, seen
    ).astype(jnp.bfloat16)
    grad_act = jnp.zeros((images, length, heads_here * VAL), jnp.float32)
    part = jnp.einsum("itd,cd->itc", grad_projected, own_rows, preferred_element_type=jnp.float32)
    grad_act = part
    act_rows = active
    weight_grad = jnp.einsum(
        "itc,itd->cd", act_rows, grad_projected, preferred_element_type=jnp.float32
    )
    grad_active = grad_act
    proj_grad = weight_grad
    grad_own = lax.dynamic_slice_in_dim(grad_view, token_start, token_share, 1)
    grad_active_groups = grad_active.reshape(groups, group_images, length, heads_here, VAL)

    def attend_back(carry, inputs):
        qkv_sum, bias_sum = carry
        block, mixed, attended, log_part, grad_act = inputs
        grad_attended = (grad_act * silu_slope(attended)).astype(jnp.bfloat16)
        weights = jnp.exp(scores_of(mixed) - log_part)
        weights_low = weights.astype(jnp.bfloat16)
        grad_weights = jnp.einsum(
            "ithc,ishc->ihts",
            grad_attended,
            mixed[..., 2 * KEY :],
            preferred_element_type=jnp.float32,
        )
        grad_scores = (
            weights * (grad_weights - jnp.sum(weights * grad_weights, axis=-1, keepdims=True))
        ).astype(jnp.bfloat16)
        bias_sum = bias_sum + jnp.sum(grad_scores.astype(jnp.float32), axis=0)
        grad_query = (
            jnp.einsum(
                "ihts,ishc->ithc",
                grad_scores,
                mixed[..., KEY : 2 * KEY],
                preferred_element_type=jnp.float32,
            )
            * scaling
        )
        grad_keys = (
            jnp.einsum(
                "ihts,ithc->ishc", grad_scores, mixed[..., :KEY], preferred_element_type=jnp.float32
            )
            * scaling
        )
        grad_values = jnp.einsum(
            "ihts,ithc->ishc", weights_low, grad_attended, preferred_element_type=jnp.float32
        )
        grad_mixed = jnp.concatenate([grad_query, grad_keys, grad_values], axis=-1).astype(
            jnp.bfloat16
        )
        qkv_sum = qkv_sum + jnp.einsum(
            "itd,ithc->hcd", block, grad_mixed, preferred_element_type=jnp.float32
        )
        return (
            (qkv_sum, bias_sum),
            jnp.einsum("ithc,hcd->itd", grad_mixed, qkv_low, preferred_element_type=jnp.float32),
        )

    start_sums = (
        jnp.zeros(qkv_weight.shape, jnp.float32),
        jnp.zeros((heads_here, length, length), jnp.float32),
    )
    (qkv_grad, bias_sum), token_terms = lax.scan(
        attend_back,
        start_sums,
        (token_groups, mixed_all, attended_all, log_total, grad_active_groups),
    )
    bias_grad = jnp.einsum("hts,tsk->hk", bias_sum, onehot, precision=lax.Precision.HIGHEST)
    tokens_grad = (
        lax.psum_scatter(
            token_terms.reshape(images, length, width).astype(jnp.bfloat16),
            "head",
            scatter_dimension=1,
            tiled=True,
        ).astype(jnp.float32)
        + grad_own
    )
    qkv_grad, bias_grad, proj_grad, up_grad, down_grad = lax.psum(
        (qkv_grad, bias_grad, proj_grad, up_grad, down_grad), "batch"
    )
    return (
        output,
        tokens_grad,
        qkv_grad,
        bias_grad,
        proj_grad,
        gain_one,
        shift_one,
        up_grad,
        gain_two,
        shift_two,
        down_grad,
        gain_three,
        shift_three,
    )


def solution(mesh):
    placed = (
        P("batch", None, None),
        P("batch"),
        P(),
        P("head", None, None),
        P("head", None),
        P(),
        P(),
        P(),
        P(None, "head"),
        P("head"),
        P("head"),
        P("head", None),
        P(),
        P(),
        P("batch", "head", None),
    )
    return jax.shard_map(
        on_device,
        mesh=mesh,
        in_specs=placed,
        out_specs=(
            P("batch", "head", None),
            P("batch", "head", None),
            P("head", None, None),
            P("head", None),
            P("head", None),
            P(),
            P(),
            P(None, "head"),
            P("head"),
            P("head"),
            P("head", None),
            P(),
            P(),
        ),
        check_vma=False,
    )
```

profile of v0, /device:TPU:0, one launch (start us, length us, event | category | flops | bytes accessed | tf_op | source)
XLA Modules:
  0.0 866.8 jit_solution(16826831131234112889)
XLA Ops:
  9.7 23.2 %fusion.35 = f32[1,196,196]{2,0,1:T(1,128)S(1)} fusion(s32[196,196]{1,0:T(8,128)S(1)} %abs_add_fusion, f32[1,196]{1,0:T(1,128)S(1)} %copy-done), kind=kOutput, calls=%fused_computation.64 | convolution fusion | flops 97883968 | bytes 308112 | tf_op jit(solution)/shard_map/hk,tsk->hts/dot_general | solution.py:60
  39.3 41.7 %while.29 = (s32[]{:T(128)}, bf16[12,4,196,1,128]{4,2,1,3,0:T(8,128)(2,1)S(1)}, f32[12,4,196,1,64]{2,4,1,3,0:T(8,128)}, f32[12,4,1,196,1]{3,1,4,2,0:T(4,128)}, b...) while((s32[]{:T(128)}, ...), condition=%wide.region_3.4_spmd, body=%wide.region_0.3_spmd.sunk | while | flops 82212592 | bytes 3833125 | solution.py:91
  87.8 71.0 %all-gather.3.cloned.1.call-done = bf16[48,196,256]{1,2,0:T(8,128)(2,1)} async-done(((bf16[48,196,64]{1,2,0:T(8,128)(2,1)}), bf16[48,196,256]{1,2,0:T(8,128)(2,1)}) %all-gather.3.cloned.1.call-update) | async-done | bytes 4816912 | tf_op jit(solution)/shard_map/all_gather | solution.py:106
  158.8 9.3 %multiply_reduce_fusion.2 = (f32[256]{0:T(256)S(1)}, f32[256]{0:T(256)S(1)}, f32[48,196,256]{2,1,0:T(8,128)}) fusion(f32[48]{0:T(128)S(1)} %compare_convert_fusion, bf16[48,196,256]{1,2,0:T(8,128)(2,1)} %all-gather.3.cloned.1.call-done, bf16[256,256]{1,0:T(8,128)(2,1)S(1)} %convert_element_type.101), kind=kOutput, calls=%fused_computation.70 | convolution fusion | flops 1245167104 | bytes 14584000 | tf_op jit(solution)/shard_map/itc,cd->itd/dot_general | solution.py:104
  168.1 16.8 %all-reduce.7 = (f32[256]{0:T(256)S(1)}, f32[]{:T(128)}, f32[256]{0:T(256)S(1)}) all-reduce(f32[256]{0:T(256)S(1)} %get-tuple-element.202, f32[]{:T(128)S(6)} %mul.367, f32[256]{0:T(256)S(1)} %get-tuple-element.201), channel_id=1, replica_groups=mesh['head'=4,'batch'=8] {'batch'}, use_global_device_ids=true, to_apply=%region_5.6 | all-reduce | flops 513 | bytes 4104 | tf_op jit(solution)/shard_map/psum | solution.py:110
  185.7 11.0 %add_add_fusion = f32[48,196,256]{2,1,0:T(8,128)} fusion(f32[48,196,256]{2,1,0:T(8,128)} %get-tuple-element.286, f32[256]{0:T(256)S(1)} %copy-done.20, f32[256]{0:T(256)S(1)} %get-tuple-element.272, f32[256]{0:T(256)S(1)} %get-tuple-element.273, f32[256]{0:T(256)S(1)} %copy-done.17, bf16[48,196,256]{2,0,1:T(8,128)(2,1)} %param.19), kind=kLoop, calls=%fused_computation.69 | loop fusion | flops 14450688 | bytes 24088576 | tf_op jit(solution)/shard_map/add | solution.py:119
  196.7 8.0 multiply_reduce_fusion.5
  204.7 14.0 %all-reduce.6 = (f32[128]{0:T(128)S(1)}, f32[128]{0:T(128)S(1)}) all-reduce(f32[128]{0:T(128)S(1)} %get-tuple-element.204, f32[128]{0:T(128)S(1)} %get-tuple-element.203), channel_id=1, replica_groups=mesh['head'=4,'batch'=8] {'batch'}, use_global_device_ids=true, to_apply=%region_11.12 | all-reduce | flops 256 | bytes 2048 | tf_op jit(solution)/shard_map/psum | solution.py:122
  229.4 55.2 %reduce-scatter.7.cloned.1.call-done = bf16[48,49,256]{2,0,1:T(8,128)(2,1)} async-done(((bf16[48,196,256]{2,0,1:T(8,128)(2,1)}), bf16[48,49,256]{2,0,1:T(8,128)(2,1)}) %reduce-scatter.7.cloned.1.call-update) | async-done | bytes 1204240
  286.8 39.4 %all-reduce.3 = (f32[256]{0:T(256)S(1)}, f32[256]{0:T(256)S(1)}) all-reduce(f32[256]{0:T(256)S(1)} %get-tuple-element.212, f32[256]{0:T(256)S(1)} %get-tuple-element.211), channel_id=1, replica_groups=mesh['head'=4,'batch'=8] {'head','batch'}, use_global_device_ids=true, to_apply=%region_16.17 | all-reduce | flops 512 | bytes 4096 | tf_op jit(solution)/shard_map/psum | solution.py:139
  329.3 40.9 %all-reduce.2 = (f32[256]{0:T(256)S(1)}, f32[256]{0:T(256)S(1)}) all-reduce(f32[256]{0:T(256)S(1)} %get-tuple-element.210, f32[256]{0:T(256)S(1)} %get-tuple-element.209), channel_id=1, replica_groups=mesh['head'=4,'batch'=8] {'head','batch'}, use_global_device_ids=true, to_apply=%region_22.23 | all-reduce | flops 512 | bytes 4096 | tf_op jit(solution)/shard_map/psum | solution.py:149
  379.1 11.2 %all-reduce.12.cloned.1.call-start = ((), (), s32[]{:S(2)}) async-start(), calls=%async_computation.4 | async-start | bytes 9830400 | tf_op jit(solution)/shard_map/psum | solution.py:191
  390.4 46.5 %all-gather.5.cloned.1.call-done = bf16[48,196,256]{2,0,1:T(8,128)(2,1)} async-done(((bf16[48,49,256]{2,0,1:T(8,128)(2,1)}), bf16[48,196,256]{2,0,1:T(8,128)(2,1)}) %all-gather.5.cloned.1.call-update) | async-done | bytes 4816912 | tf_op jit(solution)/shard_map/all_gather | solution.py:163
  436.9 10.3 %fusion.88 = (f32[128]{0:T(128)S(1)}, f32[128]{0:T(128)S(1)}, f32[48,196,128]{2,1,0:T(8,128)}) fusion(f32[128]{0:T(128)S(1)} %get-tuple-element.270, f32[48,196,128]{2,1,0:T(8,128)} %get-tuple-element.287, f32[128]{0:T(128)S(1)} %get-tuple-element.271, f32[128]{0:T(128)S(1)} %copy-done.26, f32[128]{0:T(128)S(1)} %copy-done.19, ...), kind=kOutput, calls=%fused_computation.156 | convolution fusion | flops 634658560 | bytes 14584832 | tf_op jit(solution)/shard_map/itd,fd->itf/dot_general | solution.py:165
  447.3 16.3 %all-reduce.5 = (f32[128]{0:T(128)S(1)}, f32[128]{0:T(128)S(1)}) all-reduce(f32[128]{0:T(128)S(1)} %get-tuple-element.208, f32[128]{0:T(128)S(1)} %get-tuple-element.207), channel_id=1, replica_groups=mesh['head'=4,'batch'=8] {'batch'}, use_global_device_ids=true, to_apply=%region_26.27 | all-reduce | flops 256 | bytes 2048 | tf_op jit(solution)/shard_map/psum | solution.py:172
  477.7 13.9 %dynamic_update_slice.19 = f32[48,196,256]{2,1,0:T(8,128)} dynamic-update-slice(f32[48,196,256]{2,1,0:T(8,128)} %copy-done.2, f32[48,49,256]{2,1,0:T(8,128)} %dynamic-slice_add_fusion.1, s32[]{:T(128)} %constant.49.clone.1, s32[]{:T(128)S(6)} %select_n.23, s32[]{:T(128)} %constant.49.clone.1) | dynamic-update-slice | bytes 4816900 | tf_op jit(solution)/shard_map/dynamic_update_slice | solution.py:184
  498.2 113.1 %all-reduce.12.cloned.1.call-done = bf16[48,196,256]{2,1,0:T(8,128)(2,1)} async-done(((bf16[48,196,256]{2,1,0:T(8,128)(2,1)}), bf16[48,196,256]{2,1,0:T(8,128)(2,1)}) %all-reduce.12.cloned.1.call-update) | async-done | bytes 4816912 | tf_op jit(solution)/shard_map/psum | solution.py:191
  618.6 16.3 %all-reduce.4 = (f32[256]{0:T(256)S(1)}, f32[256]{0:T(256)S(1)}) all-reduce(f32[256]{0:T(256)S(1)} %get-tuple-element.206, f32[256]{0:T(256)S(1)} %get-tuple-element.205), channel_id=1, replica_groups=mesh['head'=4,'batch'=8] {'batch'}, use_global_device_ids=true, to_apply=%region_31.32 | all-reduce | flops 512 | bytes 4096 | tf_op jit(solution)/shard_map/psum | solution.py:192
  635.6 7.5 multiply_convert_fusion.1
  648.7 84.0 %while.30 = (s32[]{:T(128)}, f32[1,128,256]{2,1,0:T(8,128)}, f32[1,196,196]{1,2,0:T(8,128)S(1)}, bf16[12,4,196,256]{3,2,1,0:T(8,128)(2,1)}, bf16[12,4,196,1,128]...) while((s32[]{:T(128)}, f32[1,128,256]{2,1,0:T(8,128)}, ...), condition=%wide.region_35.36_spmd.clone, body=%wide.region_32.35_spmd.clone.sunk | while | flops 175201728 | bytes 10991708 | solution.py:259
  738.6 8.7 %iota_compare_fusion.7 = pred[196,196,196]{2,1,0:T(8,128)(4,1)} fusion(s32[196,196]{1,0:T(8,128)S(1)} %copy-done.10), kind=kLoop, calls=%fused_computation.62.clone.clone.clone.clone.1 | loop fusion | flops 7529536 | bytes 7683200 | tf_op jit(solution)/shard_map/hts,tsk->hk/dot_general | solution.py:264
  760.2 13.3 %fusion.70 = f32[1,196]{1,0:T(1,128)S(1)} fusion(f32[196,196,1]{1,2,0:T(1,128)S(1)} %copy.77, pred[196,196,196]{2,1,0:T(8,128)(4,1)} %iota_compare_fusion.7), kind=kOutput, calls=%fused_computation.118 | convolution fusion | flops 90354432 | bytes 7683984 | tf_op jit(solution)/shard_map/hts,tsk->hk/dot_general | solution.py:264
  773.5 14.4 %psum.148 = f32[1,196]{1,0:T(1,128)} all-reduce(f32[1,196]{1,0:T(1,128)S(1)} %fusion.70), channel_id=1, replica_groups=mesh['head'=4,'batch'=8] {'batch'}, use_global_device_ids=true, to_apply=%region_38.39 | all-reduce | flops 196 | bytes 1568 | tf_op jit(solution)/shard_map/psum | solution.py:274
  804.0 49.3 %all-reduce.14.cloned.1.call-done = (f32[1,128,256]{2,1,0:T(8,128)}, f32[64,256]{1,0:T(8,128)}, f32[256,128]{1,0:T(8,128)}, f32[128,256]{1,0:T(8,128)}) async-done(((f32[1,128,256]{2,1,0:T(8,128)}, f32[64,256]{1,0:T(8,128)}, f32[256,128]{1,0:T(8,128)}, f32[128,256]{1,0:T(8,128)}), (f32[1,128,256]{2,1,0:T(8,128)}, f32[64,256]{1,0:T(8,128)}, f32[256,128]{1,0:T(8,128)}, ...) | async-done | bytes 458768 | tf_op jit(solution)/shard_map/psum | solution.py:274
  (386 shorter events, 239.7 us)
Async XLA Ops:
  7.2 151.6 %all-gather.3.cloned.1.call-start = ((), (), s32[]{:S(2)}) async-start(), calls=%async_computation.2 | async-start | bytes 7864320 | tf_op jit(solution)/shard_map/all_gather | solution.py:106
  81.0 87.2 %copy-start.12 = (bf16[12,4,196,1,128]{4,2,1,3,0:T(8,128)(2,1)}, bf16[12,4,196,1,128]{4,2,1,3,0:T(8,128)(2,1)S(1)}, u32[]{:S(2)}) copy-start(bf16[12,4,196,1,128]{4,2,1,3,0:T(8,128)(2,1)S(1)} %get-tuple-element.443) | copy-start | bytes 7225348
  85.8 198.9 %reduce-scatter.7.cloned.1.call-start = ((), (), s32[]{:S(2)}) async-start(), calls=%async_computation.5 | async-start | bytes 6021120
  87.7 97.9 %copy-start.17 = (f32[256]{0:T(256)S(1)}, f32[256]{0:T(256)}, u32[]{:S(2)}) copy-start(f32[256]{0:T(256)} %param.25) | copy-start | bytes 3076
  87.8 97.9 %copy-start.20 = (f32[256]{0:T(256)S(1)}, f32[256]{0:T(256)}, u32[]{:S(2)}) copy-start(f32[256]{0:T(256)} %param.26) | copy-start | bytes 3076
  185.7 11.0 %copy-start.11 = (f32[256,128]{1,0:T(8,128)S(1)}, f32[256,128]{1,0:T(8,128)}, u32[]{:S(2)}) copy-start(f32[256,128]{1,0:T(8,128)} %param.27) | copy-start | bytes 393220
  196.7 22.6 %copy-start.19 = (f32[128]{0:T(128)S(1)}, f32[128]{0:T(128)}, u32[]{:S(2)}) copy-start(f32[128]{0:T(128)} %param.28) | copy-start | bytes 1540
  196.7 22.6 %copy-start.26 = (f32[128]{0:T(128)S(1)}, f32[128]{0:T(128)}, u32[]{:S(2)}) copy-start(f32[128]{0:T(128)} %param.29) | copy-start | bytes 1540
  204.7 20.1 %copy-start.14 = (f32[128,256]{1,0:T(8,128)S(1)}, f32[128,256]{1,0:T(8,128)}, u32[]{:S(2)}) copy-start(f32[128,256]{1,0:T(8,128)} %param.30) | copy-start | bytes 393220
  229.3 97.5 %copy-start.5 = (bf16[48,49,256]{2,0,1:T(8,128)(2,1)S(1)}, bf16[48,49,256]{2,0,1:T(8,128)(2,1)}, u32[]{:S(2)}) copy-start(bf16[48,49,256]{2,0,1:T(8,128)(2,1)} %param.33) | copy-start | bytes 3612676
  229.3 141.5 %copy-start.18 = (f32[256]{0:T(256)S(1)}, f32[256]{0:T(256)}, u32[]{:S(2)}) copy-start(f32[256]{0:T(256)} %param.31) | copy-start | bytes 3076
  229.3 141.6 %copy-start.21 = (f32[256]{0:T(256)S(1)}, f32[256]{0:T(256)}, u32[]{:S(2)}) copy-start(f32[256]{0:T(256)} %param.32) | copy-start | bytes 3076
  229.4 207.5 %all-gather.5.cloned.1.call-start = ((), (), s32[]{:S(2)}) async-start(), calls=%async_computation.3 | async-start | bytes 6021120 | tf_op jit(solution)/shard_map/all_gather | solution.py:163
  370.2 8.8 %copy-start.22 = (f32[256]{0:T(256)}, f32[256]{0:T(256)S(1)}, u32[]{:S(2)}) copy-start(f32[256]{0:T(256)S(1)} %get-tuple-element.489) | copy-start | bytes 3076
  370.2 8.8 %copy-start.24 = (f32[256]{0:T(256)}, f32[256]{0:T(256)S(1)}, u32[]{:S(2)}) copy-start(f32[256]{0:T(256)S(1)} %get-tuple-element.490) | copy-start | bytes 3076
  379.1 232.2 %all-reduce.12.cloned.1.call-start = ((), (), s32[]{:S(2)}) async-start(), calls=%async_computation.4 | async-start | bytes 9830400 | tf_op jit(solution)/shard_map/psum | solution.py:191
  498.1 301.0 %reduce-scatter.9.cloned.1.call-start = ((), (), s32[]{:S(2)}) async-start(), calls=%async_computation.6 | async-start | bytes 6021120
  634.9 8.2 copy-start.25
  738.3 115.0 %all-reduce.14.cloned.1.call-start = ((), (), s32[]{:S(2)}) async-start(), calls=%async_computation.7 | async-start | bytes 917504 | tf_op jit(solution)/shard_map/psum | solution.py:274
  738.6 19.1 %slice-start = ((s8[9830400]{0:T(1024)(128)(4,1)}), s8[4194304]{0:T(1024)(128)(4,1)S(1)}, s32[]{:S(2)}) async-start(s8[9830400]{0:T(1024)(128)(4,1)} %bitcast.244), calls=%async_computation.8 | async-start | bytes 8388608
  738.6 19.1 %slice-start.1 = ((s8[9830400]{0:T(1024)(128)(4,1)}), s8[4194304]{0:T(1024)(128)(4,1)S(1)}, s32[]{:S(2)}) async-start(s8[9830400]{0:T(1024)(128)(4,1)} %bitcast.244), calls=%async_computation.9 | async-start | bytes 8388608
  747.3 10.4 %slice-start.2 = ((s8[9830400]{0:T(1024)(128)(4,1)}), s8[1441792]{0:T(1024)(128)(4,1)S(1)}, s32[]{:S(2)}) async-start(s8[9830400]{0:T(1024)(128)(4,1)} %bitcast.244), calls=%async_computation.10 | async-start | bytes 2883584
  760.2 27.7 %copy-start.4 = (bf16[12,4,196,1,64]{2,4,1,3,0:T(8,128)(2,1)S(1)}, bf16[12,4,196,1,64]{2,4,1,3,0:T(8,128)(2,1)}, u32[]{:S(2)}) copy-start(bf16[12,4,196,1,64]{2,4,1,3,0:T(8,128)(2,1)} %multiply_convert_fusion.4) | copy-start | bytes 3612676
  791.9 67.6 %copy-start.1 = (f32[1,196]{1,0:T(1,128)S(1)}, f32[1,196]{1,0:T(1,128)}, u32[]{:S(2)}) copy-start(f32[1,196]{1,0:T(1,128)} %param.23) | copy-start | bytes 2356
  (36 other events, 86.2 us)
Sparse Core Ops, SparseCore 0:
  85.9 72.8 all-gather.2
  229.5 55.1 reduce-scatter.6
  379.2 57.6 all-gather.4
  498.2 112.9 all-reduce.11
  738.4 55.1 reduce-scatter.8
  797.2 56.1 all-reduce.13
where the time goes:
time: 878 us; the launch traced here: 867 us
  waiting for transfers between devices  335 us (38%)
  matrix products  161 us (18%)
  blocking collectives  158 us (18%)
  other arithmetic  111 us (13%)
  local copies, waits for them, and re-layouts  72.8 us (8%)
  between operations  16.3 us (2%)
  starting transfers between devices  11.6 us (1%)
    psum x1, waiting for transfers between devices, on_device(): lax.psum(grad_residual.astype(jnp.bfloat16), 'head').astype(jnp.float32)  113 us
    all_gather x1, waiting for transfers between devices, on_device(): lax.all_gather(active, 'head', axis=2, tiled=True)  71 us
    unnamed x8, waiting for transfers between devices  55.3 us
    psum x1, waiting for transfers between devices, on_device(): lax.psum((qkv_grad, bias_grad, proj_grad, up_grad, down_grad), 'batch')  49.3 us
    all_gather x1, waiting for transfers between devices, on_device(): piece = lax.all_gather(grad_outgoing, 'head', axis=1, tiled=True)  46.5 us
    psum x1, blocking collectives, on_device(): lax.psum((jnp.sum(upstream, axis=(0, 1)), jnp.sum(upstream * normed_three...  40.9 us
    psum x1, blocking collectives, on_device(): lax.psum((jnp.sum(outgoing * rows_valid, axis=(0, 1)), jnp.sum(outgoing *...  39.4 us
    unnamed x67, local copies, waits for them, and re-layouts  26.8 us
  transfers between devices with their start and end apart: 6, of which 5 were waited for; matrix products, arithmetic and copies ran while one was open for 6% of the time, Pallas kernels for 0%

commit v1 on v0

v1 whole, which is shorter than its diff:
```python
import functools
import types

import jax
import jax.numpy as jnp
from jax import lax
from jax.experimental import pallas as pl
from jax.experimental.pallas import tpu as pltpu
from jax.sharding import PartitionSpec as P

KEY = 32
VAL = 64
SIDE = 14
EPSILON = 1e-05
LOG2E = 1.4426950408889634
MESH = pl.DeviceIdType.MESH
f32 = jnp.float32
bf16 = jnp.bfloat16


def nn(left, right):
    return lax.dot_general(left, right, (((1,), (0,)), ((), ())), preferred_element_type=f32)


def nt(left, right):
    return lax.dot_general(left, right, (((1,), (1,)), ((), ())), preferred_element_type=f32)


def round_up(value, step):
    return -(-value // step) * step


def sigmoid(value):
    return 0.5 * jnp.tanh(0.5 * value) + 0.5


def fold(value):
    rows, columns = value.shape
    return jnp.sum(value.reshape(rows // 8, 8, columns), axis=0)


def total(value):
    return jnp.sum(value, axis=0, keepdims=True)


def lookup(table, index):
    rows = index.shape[0]
    low = jnp.broadcast_to(table[:, 0:128], (rows, 128))
    high = jnp.broadcast_to(table[:, 128:256], (rows, 128))
    return take(low, high, index)


def take(low, high, index):
    parts = []
    for half in range(2):
        at = index[:, half * 128 : (half + 1) * 128]
        inside = lax.bitwise_and(at, 127)
        first = jnp.take_along_axis(low, inside, axis=1, mode="promise_in_bounds")
        second = jnp.take_along_axis(high, inside, axis=1, mode="promise_in_bounds")
        parts.append(jnp.where(at < 128, first, second))
    return jnp.concatenate(parts, axis=1)


def layout(z):
    n, T, L, D, F, H, B, C = z.n, z.T, z.L, z.D, z.F, z.H, z.B, z.C
    dma = pltpu.SemaphoreType.DMA
    vmem = pltpu.VMEM
    return {
        "qkv32": vmem((C, D), f32),
        "up32": vmem((D, F // H), f32),
        "down32": vmem((F // H, D), f32),
        "proj32": vmem((D, D), f32),
        "xraw": vmem((n, z.length, D), bf16),
        "qkvg": vmem((H, C, D), bf16),
        "upg": vmem((H, D, F // H), bf16),
        "downg": vmem((H, F // H, D), bf16),
        "smallg": vmem((H, 4, 128), f32),
        "ct": vmem((H, n, z.share, D), bf16),
        "w2": vmem((H * C, D), bf16),
        "w2t": vmem((D, H * C), bf16),
        "upcat": vmem((D, F), bf16),
        "projw": vmem((D, D), bf16),
        "bias": vmem((H, T, L), f32),
        "dbias": vmem((H, T, L), f32),
        "rowmask": vmem((T, D), f32),
        "eye": vmem((D, D), bf16),
        "eyet": vmem((T, L), bf16),
        "onehot": vmem((L, L), bf16),
        "xpad": vmem((n, L, D), bf16),
        "mt": vmem((n, H * C, L), bf16),
        "vnat": vmem((n, T, H * VAL), bf16),
        "qbd": vmem((H * KEY, H * L), bf16),
        "dabd": vmem((H * VAL, H * L), bf16),
        "p": vmem((n, H, T, L), bf16),
        "linv": vmem((n, H, 1, L), f32),
        "att": vmem((n, H * VAL, L), f32),
        "act": vmem((n, H * VAL, L), bf16),
        "proj": vmem((n, T, D), f32),
        "res": vmem((n, T, D), bf16),
        "hid": vmem((n, T, F), f32),
        "slope": vmem((n, T, F), f32),
        "act2": vmem((n, T, F), bf16),
        "out": vmem((n, T, D), f32),
        "u": vmem((n, T, D), f32),
        "gproj": vmem((n, L, D), bf16),
        "tmp": vmem((T, D), f32),
        "osend": vmem((H, n, z.share, D), bf16),
        "dmt": vmem((H * C, L), bf16),
        "gdown": vmem((D, F), f32),
        "gup": vmem((D, F), f32),
        "gpr": vmem((D, D), f32),
        "gqkv": vmem((H * C, D), f32),
        "srow": vmem((2, F), f32),
        "ar0h": vmem((H, 4, D), f32),
        "ar0b": vmem((B, 4, D), f32),
        "ar1h": vmem((H, 2, F), f32),
        "ar1b": vmem((B, 2, F), f32),
        "ar2h": vmem((H, 4, D), f32),
        "ar2b": vmem((B, 4, D), f32),
        "ar3h": vmem((H, 2, F), f32),
        "ar3b": vmem((B, 2, F), f32),
        "ar4h": vmem((H, 2, D), f32),
        "ar4b": vmem((B, 2, D), f32),
        "ar5h": vmem((H, H, L), f32),
        "ar5b": vmem((B, H, L), f32),
        "ge1": vmem((H, z.re, 128), bf16),
        "ge1r": vmem((H, z.re, 128), bf16),
        "ge2": vmem((B, z.re // B, 128), f32),
        "ge2r": vmem((B, z.re // B, 128), f32),
        "ge3": vmem((B, z.re // B, 128), f32),
        "gl1": vmem((H, z.rl, 128), bf16),
        "gl1r": vmem((H, z.rl, 128), bf16),
        "gl2": vmem((B, z.rl // B, 128), f32),
        "gl2r": vmem((B, z.rl // B, 128), f32),
        "gl3": vmem((B, z.rl // B, 128), f32),
        "loc": dma((8,)),
        "hs": dma((9, H)),
        "hr": dma((9, H)),
        "ahs": dma((6, H)),
        "ahr": dma((6, H)),
        "abs": dma((6, B)),
        "abr": dma((6, B)),
        "gbs": dma((4, B)),
        "gbr": dma((4, B)),
    }


def block_kernel(z, names, *refs):
    (tokens, count, place, qkv_w, table, proj_w, gain_1, shift_1, up_w, gain_2, shift_2, down_w,
     gain_3, shift_3, cot, out_o, tg_o, early_o, late_o, small_o) = refs[:20]
    s = types.SimpleNamespace(**dict(zip(names, refs[20:], strict=True)))
    n, T, L, D, F, H, B, C = z.n, z.T, z.L, z.D, z.F, z.H, z.B, z.C
    share, length = z.share, z.length
    me_h = lax.axis_index("head")
    me_b = lax.axis_index("batch")

    def local(src, dst, k):
        copy = pltpu.make_async_copy(src, dst, s.loc.at[k])
        copy.start()
        return copy

    def to_head(src, dst, k, j):
        return pltpu.make_async_remote_copy(
            src_ref=src, dst_ref=dst, send_sem=s.hs.at[k, j], recv_sem=s.hr.at[k, j],
            device_id={"head": lax.rem(me_h + j, H)}, device_id_type=MESH)

    def to_batch(src, dst, send, recv, j):
        return pltpu.make_async_remote_copy(
            src_ref=src, dst_ref=dst, send_sem=send, recv_sem=recv,
            device_id={"batch": lax.rem(me_b + j, B)}, device_id_type=MESH)

    def around(size, step):
        if size <= 8:
            for j in range(1, size):
                step(j)
        else:
            lax.fori_loop(1, size, lambda j, c: (step(j), c)[1], 0)

    c_qkv = local(qkv_w.at[0], s.qkv32, 0)
    c_up = local(up_w, s.up32, 1)
    c_down = local(down_w, s.down32, 2)
    c_tok = local(tokens.at[pl.ds(me_h * n, n)], s.xraw, 3)
    c_proj = local(proj_w, s.proj32, 4)

    barrier = pltpu.get_barrier_semaphore()
    around(H, lambda j: pl.semaphore_signal(
        barrier, inc=1, device_id={"head": lax.rem(me_h + j, H)}, device_id_type=MESH))
    around(B, lambda j: pl.semaphore_signal(
        barrier, inc=1, device_id={"batch": lax.rem(me_b + j, B)}, device_id_type=MESH))

    s.smallg[me_h] = jnp.concatenate(
        [gain_2[...], shift_2[...], table[:, 0:128], jnp.concatenate(
            [table[:, 128:length], jnp.zeros((1, 256 - length), f32)], axis=1)], axis=0)
    c_qkv.wait()
    s.qkvg[me_h] = s.qkv32[...].astype(bf16)
    c_up.wait()
    s.upg[me_h] = s.up32[...].astype(bf16)
    c_down.wait()
    s.downg[me_h] = s.down32[...].astype(bf16)

    pl.semaphore_wait(barrier, H - 1 + B - 1)

    weights = (s.qkvg, s.smallg, s.upg, s.downg)
    for k in range(2):
        for j in range(1, H):
            to_head(weights[k].at[me_h], weights[k].at[me_h], k, j).start()
    for k in range(2, 4):
        for j in range(1, H):
            to_head(weights[k].at[me_h], weights[k].at[me_h], k, j).start()
    for j in range(1, H):
        to_head(cot.at[pl.ds(lax.rem(me_h + j, H) * n, n)], s.ct.at[me_h], 4, j).start()
    c_cot = local(cot.at[pl.ds(me_h * n, n)], s.ct.at[me_h], 5)

    row_at = lax.broadcasted_iota(jnp.int32, (L, L), 0)
    lane_at = lax.broadcasted_iota(jnp.int32, (L, L), 1)
    s.eye[...] = jnp.where(row_at == lane_at, 1.0, 0.0).astype(bf16)
    s.eyet[...] = jnp.where((row_at == lane_at) & (row_at < length), 1.0, 0.0)[0:T].astype(bf16)
    s.rowmask[...] = jnp.where(row_at < length, 1.0, 0.0)[0:T]
    place_lane = jnp.broadcast_to(
        jnp.concatenate([place[...].astype(f32), jnp.zeros((1, L - length), f32)], axis=1), (L, L))
    place_row = place_lane.T
    s.onehot[...] = jnp.where((place_row == lane_at.astype(f32)) & (row_at < length), 1.0, 0.0).astype(bf16)

    def grid_of(at):
        at = at.astype(jnp.int32)
        row = lax.shift_right_logical(at * 4682, 16)
        return row, at - row * SIDE

    rows_t, cols_t = grid_of(place_lane[0:T])
    rows_s, cols_s = grid_of(place_row[0:T])
    offsets = jnp.abs(rows_s - rows_t) * SIDE + jnp.abs(cols_s - cols_t)
    for h in range(H):
        s.dbias[h] = jnp.zeros((T, L), f32)
    s.qbd[...] = jnp.zeros(s.qbd.shape, bf16)
    s.dabd[...] = jnp.zeros(s.dabd.shape, bf16)
    s.dmt[...] = jnp.zeros(s.dmt.shape, bf16)
    s.gdown[...] = jnp.zeros(s.gdown.shape, f32)
    s.gup[...] = jnp.zeros(s.gup.shape, f32)
    s.gpr[...] = jnp.zeros(s.gpr.shape, f32)
    s.gqkv[...] = jnp.zeros(s.gqkv.shape, f32)

    def valid_of(i):
        return jnp.where(me_h * n + i < count[0], 1.0, 0.0)

    c_proj.wait()
    s.projw[...] = s.proj32[...].astype(bf16)
    c_tok.wait()

    def pad(i, carry):
        s.xpad[i] = jnp.zeros((L, D), bf16)
        s.xpad[i, 0:length, :] = (s.xraw[i].astype(f32) * valid_of(i)).astype(bf16)
        s.gproj[i, T:L, :] = jnp.zeros((L - T, D), bf16)
        return carry

    lax.fori_loop(0, n, pad, 0)

    for k in range(2):
        for j in range(1, H):
            to_head(weights[k].at[me_h], weights[k].at[me_h], k, j).wait()
    for h in range(H):
        s.w2[h * KEY : (h + 1) * KEY] = s.qkvg[h, 0:KEY]
        s.w2[(H + h) * KEY : (H + h + 1) * KEY] = s.qkvg[h, KEY : 2 * KEY]
        at = 2 * H * KEY + h * VAL
        s.w2[at : at + VAL] = s.qkvg[h, 2 * KEY : C]
        line = jnp.concatenate([s.smallg[h, 2:3, :], s.smallg[h, 3:4, :]], axis=1)
        s.bias[h] = jnp.where(row_at[0:T] < length, lookup(line, offsets) * LOG2E, -1e30)

    scale = KEY**-0.5
    KH, VH = H * KEY, H * VAL

    def attend(i, carry):
        first, second = carry
        x = s.xpad[i]
        mixed = nt(s.w2[...], x).astype(bf16)
        s.mt[i] = mixed
        natural = nt(x[0:T], s.w2[KH : H * C]).astype(bf16)
        s.vnat[i] = natural[:, KH:]
        keys = natural[:, 0:KH]
        for h in range(H):
            s.qbd[h * KEY : (h + 1) * KEY, h * L : (h + 1) * L] = mixed[h * KEY : (h + 1) * KEY]
        for h in range(H):
            scores = nn(keys, s.qbd[:, h * L : (h + 1) * L]) * (scale * LOG2E) + s.bias[h]
            raised = jnp.exp2(scores - jnp.max(scores, axis=0, keepdims=True))
            inverse = 1.0 / total(raised)
            s.linv[i, h] = inverse
            low = raised.astype(bf16)
            s.p[i, h] = low
            values = mixed[2 * KH + h * VAL : 2 * KH + (h + 1) * VAL, 0:T]
            attended = nn(values, low) * inverse
            s.att[i, h * VAL : (h + 1) * VAL] = attended
            s.act[i, h * VAL : (h + 1) * VAL] = (attended * sigmoid(attended)).astype(bf16)
        active = nt(s.eyet[...], s.act[i]).astype(bf16)
        projected = nn(active, s.projw[...])
        s.proj[i] = projected
        return first + fold(projected), second + fold(projected * projected)

    def zeros(width):
        return jnp.zeros((8, width), f32)

    def all_reduce(k, rows, hbuf, bbuf):
        for r, row in enumerate(rows):
            hbuf[me_h, r : r + 1, :] = row
        for j in range(1, H):
            pltpu.make_async_remote_copy(
                src_ref=hbuf.at[me_h], dst_ref=hbuf.at[me_h], send_sem=s.ahs.at[k, j], recv_sem=s.ahr.at[k, j],
                device_id={"head": lax.rem(me_h + j, H)}, device_id_type=MESH).start()
        for j in range(1, H):
            pltpu.make_async_remote_copy(
                src_ref=hbuf.at[me_h], dst_ref=hbuf.at[me_h], send_sem=s.ahs.at[k, j], recv_sem=s.ahr.at[k, j],
                device_id={"head": lax.rem(me_h + j, H)}, device_id_type=MESH).wait()
        part = hbuf[0]
        for h in range(1, H):
            part = part + hbuf[h]
        bbuf[me_b] = part
        around(B, lambda j: to_batch(bbuf.at[me_b], bbuf.at[me_b], s.abs.at[k, j], s.abr.at[k, j], j).start())
        around(B, lambda j: to_batch(bbuf.at[me_b], bbuf.at[me_b], s.abs.at[k, j], s.abr.at[k, j], j).wait())
        if B <= 8:
            whole = bbuf[0]
            for b in range(1, B):
                whole = whole + bbuf[b]
            return whole
        return lax.fori_loop(1, B, lambda b, c: c + bbuf[b], bbuf[0])

    first, second = lax.fori_loop(0, n, attend, (zeros(D), zeros(D)))
    mine = jnp.clip(count[0] - me_h * n, 0, n).astype(f32) * float(length)
    sums = all_reduce(
        0, [total(first), total(second), jnp.full((1, D), mine), jnp.zeros((1, D), f32)], s.ar0h, s.ar0b)
    seen_row = sums[2:3, :]
    seen_wide = jnp.concatenate([seen_row] * (F // D), axis=1)

    def moments(first, second, seen):
        mean = first / seen
        return mean, lax.rsqrt(second / seen - mean * mean + EPSILON)

    mean_1, inverse_1 = moments(sums[0:1], sums[1:2], seen_row)
    a_1 = gain_1[...] * inverse_1
    b_1 = shift_1[...] - mean_1 * a_1

    for k in range(2, 4):
        for j in range(1, H):
            to_head(weights[k].at[me_h], weights[k].at[me_h], k, j).wait()
    for h in range(H):
        s.upcat[:, h * (F // H) : (h + 1) * (F // H)] = s.upg[h]
    down = s.downg[...].reshape(F, D)

    def residual_of(i):
        return s.xpad[i, 0:T].astype(f32) + (s.proj[i] * a_1 + (b_1 * valid_of(i)) * s.rowmask[...])

    def enter(i, carry):
        first, second = carry
        residual = residual_of(i).astype(bf16)
        s.res[i] = residual
        hidden = nn(residual, s.upcat[...])
        s.hid[i] = hidden
        return first + fold(hidden), second + fold(hidden * hidden)

    first, second = lax.fori_loop(0, n, enter, (zeros(F), zeros(F)))
    sums = all_reduce(1, [total(first), total(second)], s.ar1h, s.ar1b)
    mean_2, inverse_2 = moments(sums[0:1], sums[1:2], seen_wide)
    gain_2w = jnp.concatenate([s.smallg[h, 0:1, :] for h in range(H)], axis=1)
    shift_2w = jnp.concatenate([s.smallg[h, 1:2, :] for h in range(H)], axis=1)
    a_2 = gain_2w * inverse_2
    b_2 = shift_2w - mean_2 * a_2

    for j in range(1, H):
        to_head(cot.at[pl.ds(lax.rem(me_h + j, H) * n, n)], s.ct.at[me_h], 4, j).wait()
    c_cot.wait()

    def leave(i, carry):
        one, two, three, four = carry
        shaped = s.hid[i] * a_2 + b_2
        gate = sigmoid(shaped)
        active = shaped * gate
        s.slope[i] = gate + active * (1.0 - gate)
        low = active.astype(bf16)
        s.act2[i] = low
        outgoing = nn(low, down)
        s.out[i] = outgoing
        valid = valid_of(i)
        s.u[i, T - 16 : T, :] = jnp.zeros((16, D), f32)
        for q in range(H):
            s.u[i, q * share : (q + 1) * share, :] = s.ct[q, i].astype(f32) * valid
        upstream = s.u[i]
        masked = outgoing * (s.rowmask[...] * valid)
        return (one + fold(masked), two + fold(masked * outgoing), three + fold(upstream),
                four + fold(upstream * outgoing))

    sums = lax.fori_loop(0, n, leave, (zeros(D), zeros(D), zeros(D), zeros(D)))
    sums = all_reduce(2, [total(v) for v in sums], s.ar2h, s.ar2b)
    mean_3, inverse_3 = moments(sums[0:1], sums[1:2], seen_row)
    a_3 = gain_3[...] * inverse_3
    b_3 = shift_3[...] - mean_3 * a_3
    sum_shift_3 = sums[2:3]
    sum_gain_3 = inverse_3 * (sums[3:4] - mean_3 * sum_shift_3)

    def back(gain, mean, inverse, sum_shift, sum_gain, seen):
        scaled = gain * inverse
        slope = -scaled * inverse * (sum_gain / seen)
        return scaled, slope, -scaled * (sum_shift / seen) - slope * mean

    s_3, v_3, r_3 = back(gain_3[...], mean_3, inverse_3, sum_shift_3, sum_gain_3, seen_row)

    def back_leave(i, carry):
        one, two = carry
        valid = valid_of(i)
        outgoing = s.out[i]
        s.tmp[...] = (residual_of(i) + (outgoing * a_3 + b_3)) * valid
        for q in range(H):
            s.osend[q, i] = s.tmp[q * share : (q + 1) * share, :].astype(bf16)
        grad = (s.u[i] * s_3 + (outgoing * v_3 + r_3) * (s.rowmask[...] * valid)).astype(bf16)
        shaped = nt(grad, down) * s.slope[i]
        s.slope[i] = shaped
        turned = nt(s.eye[...], grad).astype(bf16)
        s.gdown[...] += nn(turned, s.act2[i])
        return one + fold(shaped), two + fold(shaped * s.hid[i])

    first, second = lax.fori_loop(0, n, back_leave, (zeros(F), zeros(F)))
    sums = all_reduce(3, [total(first), total(second)], s.ar3h, s.ar3b)

    for j in range(1, H):
        to_head(s.osend.at[lax.rem(me_h + j, H)], out_o.at[pl.ds(me_h * n, n)], 5, j).start()
    c_out = local(s.osend.at[me_h], out_o.at[pl.ds(me_h * n, n)], 6)

    sum_shift_2 = sums[0:1]
    sum_gain_2 = inverse_2 * (sums[1:2] - mean_2 * sum_shift_2)
    s_2, v_2, r_2 = back(gain_2w, mean_2, inverse_2, sum_shift_2, sum_gain_2, seen_wide)
    s.srow[0:1, :] = sum_gain_2
    s.srow[1:2, :] = sum_shift_2

    def back_enter(i, carry):
        one, two = carry
        mask = s.rowmask[...] * valid_of(i)
        grad = (s.slope[i] * s_2 + s.hid[i] * v_2 + r_2 * jnp.concatenate([mask] * (F // D), axis=1)).astype(bf16)
        turned = nt(s.eye[...], s.res[i]).astype(bf16)
        s.gup[...] += nn(turned, grad)
        upstream = s.u[i] + nt(grad, s.upcat[...])
        s.u[i] = upstream
        return one + fold(upstream), two + fold(upstream * s.proj[i])

    first, second = lax.fori_loop(0, n, back_enter, (zeros(D), zeros(D)))
    sums = all_reduce(4, [total(first), total(second)], s.ar4h, s.ar4b)
    sum_shift_1 = sums[0:1]
    sum_gain_1 = inverse_1 * (sums[1:2] - mean_1 * sum_shift_1)
    s_1, v_1, r_1 = back(gain_1[...], mean_1, inverse_1, sum_shift_1, sum_gain_1, seen_row)

    def back_project(i, carry):
        mask = s.rowmask[...] * valid_of(i)
        grad = (s.u[i] * s_1 + s.proj[i] * v_1 + r_1 * mask).astype(bf16)
        s.gproj[i, 0:T, :] = grad
        s.gpr[...] += nn(s.act[i], s.gproj[i])
        return carry

    lax.fori_loop(0, n, back_project, 0)

    def shares(buffer, k):
        for j in range(1, H):
            yield to_head(buffer[0].at[lax.rem(me_h + j, H)], buffer[1].at[me_h], k, j)

    def head_sum(buffer):
        whole = buffer[0][me_h].astype(f32)
        for j in range(1, H):
            whole = whole + buffer[1][lax.rem(me_h + j, H)].astype(f32)
        return whole

    def spread(src, dst, k, act):
        around(B, lambda j: act(to_batch(src(lax.rem(me_b + j, B)), dst, s.gbs.at[k, j], s.gbr.at[k, j], j)))

    def batch_sum(own, received):
        if B <= 8:
            whole = own
            for j in range(1, B):
                whole = whole + received[lax.rem(me_b + j, B)]
            return whole
        return lax.fori_loop(1, B, lambda j, c: c + received[lax.rem(me_b + j, B)], own)

    FH = F // H
    PH = D // H
    for h in range(H):
        s.ge1[h, 0:D, :] = s.gup[:, h * FH : (h + 1) * FH].astype(bf16)
        s.ge1[h, D : 2 * D, :] = s.gdown[:, h * FH : (h + 1) * FH].astype(bf16)
        for half in range(D // 128):
            at = 2 * D + half * PH
            s.ge1[h, at : at + PH, :] = s.gpr[h * PH : (h + 1) * PH, half * 128 : (half + 1) * 128].astype(bf16)
        if z.re > 2 * D + PH * (D // 128):
            s.ge1[h, 2 * D + PH * (D // 128) :, :] = jnp.zeros((z.re - 2 * D - PH * (D // 128), 128), bf16)
    for copy in shares((s.ge1, s.ge1r), 7):
        copy.start()

    for j in range(1, H):
        to_head(s.osend.at[lax.rem(me_h + j, H)], out_o.at[pl.ds(me_h * n, n)], 5, j).wait()
    c_out.wait()

    def back_attend(i, carry):
        slope_gate = sigmoid(s.att[i])
        att = s.att[i]
        active = att * slope_gate
        gact = nt(s.projw[...], s.gproj[i]) * (slope_gate + active * (1.0 - slope_gate))
        for h in range(H):
            rows = slice(h * VAL, (h + 1) * VAL)
            grad = gact[rows] * s.linv[i, h]
            low = grad.astype(bf16)
            s.dabd[rows, h * L : (h + 1) * L] = low
            delta = total(grad * att[rows])
            weights_low = s.p[i, h]
            gscores = weights_low.astype(f32) * (nn(s.vnat[i], s.dabd[:, h * L : (h + 1) * L]) - delta)
            s.dbias[h] += gscores
            glow = gscores.astype(bf16)
            q_rows = slice(h * KEY, (h + 1) * KEY)
            k_rows = slice(KH + h * KEY, KH + (h + 1) * KEY)
            v_rows = slice(2 * KH + h * VAL, 2 * KH + (h + 1) * VAL)
            s.dmt[q_rows, :] = (nn(s.mt[i, k_rows, 0:T], glow) * scale).astype(bf16)
            s.dmt[k_rows, 0:T] = (nt(s.mt[i, q_rows, :], glow) * scale).astype(bf16)
            s.dmt[v_rows, 0:T] = nt(low, weights_low).astype(bf16)
        s.gqkv[...] += nn(s.dmt[...], s.xpad[i])
        turned = nn(s.w2t[...], s.dmt[...]).astype(bf16)
        s.tmp[...] = s.u[i] + nt(s.eyet[...], turned)
        for q in range(H):
            s.osend[q, i] = s.tmp[q * share : (q + 1) * share, :].astype(bf16)
        for j in range(1, H):
            to_head(s.osend.at[lax.rem(me_h + j, H), i], tg_o.at[me_h * n + i], 6, j).start()
        pltpu.make_async_copy(s.osend.at[me_h, i], tg_o.at[me_h * n + i], s.loc.at[7]).start()
        return carry

    s.w2t[...] = nt(s.eye[...], s.w2[...]).astype(bf16)
    lax.fori_loop(0, n // 2, back_attend, 0)

    for copy in shares((s.ge1, s.ge1r), 7):
        copy.wait()
    s.ge2[...] = head_sum((s.ge1, s.ge1r)).reshape(B, z.re // B, 128)
    spread(lambda peer: s.ge2.at[peer], s.ge2r.at[me_b], 0, lambda c: c.start())

    lax.fori_loop(n // 2, n, back_attend, 0)

    spread(lambda peer: s.ge2.at[peer], s.ge2r.at[me_b], 0, lambda c: c.wait())
    s.ge3[me_b] = batch_sum(s.ge2[me_b], s.ge2r)
    spread(lambda peer: s.ge3.at[me_b], s.ge3.at[me_b], 1, lambda c: c.start())

    for h in range(H):
        for half in range(D // 128):
            lanes = slice(half * 128, (half + 1) * 128)
            at = half * C
            s.gl1[h, at : at + KEY, :] = s.gqkv[h * KEY : (h + 1) * KEY, lanes].astype(bf16)
            s.gl1[h, at + KEY : at + 2 * KEY, :] = s.gqkv[KH + h * KEY : KH + (h + 1) * KEY, lanes].astype(bf16)
            s.gl1[h, at + 2 * KEY : at + C, :] = s.gqkv[2 * KH + h * VAL : 2 * KH + (h + 1) * VAL, lanes].astype(bf16)
        if z.rl > C * (D // 128):
            s.gl1[h, C * (D // 128) :, :] = jnp.zeros((z.rl - C * (D // 128), 128), bf16)
    for copy in shares((s.gl1, s.gl1r), 8):
        copy.start()

    slot = lax.broadcasted_iota(jnp.int32, (T, L), 1)
    d_row, d_col = grid_of(slot)
    picks = []
    for down_sign in (1, -1):
        for right_sign in (1, -1):
            r = rows_s + down_sign * d_row
            c = cols_s + right_sign * d_col
            good = (r >= 0) & (r < SIDE) & (c >= 0) & (c < SIDE) & (slot < length)
            if down_sign < 0:
                good = good & (d_row > 0)
            if right_sign < 0:
                good = good & (d_col > 0)
            picks.append((jnp.where(good, r * SIDE + c, 0), good))
    bias_rows = []
    for h in range(H):
        whole = s.dbias[h]
        high = whole.astype(bf16)
        rest = (whole - high.astype(f32)).astype(bf16)
        ordered = nn(high, s.onehot[...]) + nn(rest, s.onehot[...])
        line = jnp.zeros((T, L), f32)
        for index, good in picks:
            line = line + jnp.where(good, take(ordered[:, 0:128], ordered[:, 128:256], index), 0.0)
        bias_rows.append(total(line * s.rowmask[...]))
    bias_sums = all_reduce(5, bias_rows, s.ar5h, s.ar5b)
    s.ar5h[0] = bias_sums

    for copy in shares((s.gl1, s.gl1r), 8):
        copy.wait()
    s.gl2[...] = head_sum((s.gl1, s.gl1r)).reshape(B, z.rl // B, 128)
    spread(lambda peer: s.gl2.at[peer], s.gl2r.at[me_b], 2, lambda c: c.start())
    spread(lambda peer: s.gl2.at[peer], s.gl2r.at[me_b], 2, lambda c: c.wait())
    s.gl3[me_b] = batch_sum(s.gl2[me_b], s.gl2r)
    spread(lambda peer: s.gl3.at[me_b], s.gl3.at[me_b], 3, lambda c: c.start())

    own = pl.ds(pl.multiple_of(me_h * FH, FH), FH)
    small_o[...] = jnp.zeros(small_o.shape, f32)
    small_o[0:1, :] = sum_gain_1
    small_o[1:2, :] = sum_shift_1
    small_o[2:3, :] = sum_gain_3
    small_o[3:4, :] = sum_shift_3
    small_o[4:5, 0:FH] = s.srow[0:1, own]
    small_o[5:6, 0:FH] = s.srow[1:2, own]
    small_o[6:7, :] = s.ar5h[0, pl.ds(me_h, 1), :]

    spread(lambda peer: s.ge3.at[me_b], s.ge3.at[me_b], 1, lambda c: c.wait())
    early_o[...] = s.ge3[...].reshape(z.re, 128)
    spread(lambda peer: s.gl3.at[me_b], s.gl3.at[me_b], 3, lambda c: c.wait())
    late_o[...] = s.gl3[...].reshape(z.rl, 128)

    for j in range(1, H):
        to_head(s.osend.at[lax.rem(me_h + j, H)], tg_o.at[pl.ds(me_h * n, n)], 6, j).wait()
    pltpu.make_async_copy(s.osend.at[me_h], tg_o.at[pl.ds(me_h * n, n)], s.loc.at[7]).wait()


def finish_kernel(z, out_i, tg_i, early, late, small, out, tg, qkv, bias, proj, g1, s1, up, g2, s2, down, g3, s3):
    out[...] = out_i[...].astype(f32)
    tg[...] = tg_i[...].astype(f32)

    @pl.when(pl.program_id(0) == 0)
    def _():
        D, C, PH = z.D, z.C, z.D // z.H
        up[...] = early[0:D, :]
        down[...] = early[D : 2 * D, :].T
        for half in range(D // 128):
            lanes = slice(half * 128, (half + 1) * 128)
            proj[:, lanes] = early[2 * D + half * PH : 2 * D + (half + 1) * PH, :]
            qkv[0, :, lanes] = late[half * C : (half + 1) * C, :]
        g1[...] = small[0:1, :]
        s1[...] = small[1:2, :]
        g3[...] = small[2:3, :]
        s3[...] = small[3:4, :]
        g2[...] = small[4:5, 0 : z.F // z.H]
        s2[...] = small[5:6, 0 : z.F // z.H]
        bias[...] = small[6:7, 0 : z.length]


def on_device(H, B, tokens, image_count, token_place, qkv_weight, bias_table, proj_weight, attention_gain,
              attention_shift, up_weight, hidden_gain, hidden_shift, down_weight, output_gain, output_shift,
              cotangent):
    images, length, width = tokens.shape
    z = types.SimpleNamespace(
        n=images // H, T=round_up(length, 16), L=round_up(length, 128), D=width, F=up_weight.shape[1] * H,
        H=H, B=B, C=qkv_weight.shape[1], share=cotangent.shape[1], length=length)
    z.re = round_up(2 * z.D + z.D // H * (z.D // 128), 8 * max(B, 2))
    z.rl = round_up(z.C * (z.D // 128), 8 * max(B, 2))
    scratch = layout(z)
    hbm = pl.BlockSpec(memory_space=pl.ANY)
    vmem = pl.BlockSpec(memory_space=pltpu.VMEM)
    smem = pl.BlockSpec(memory_space=pltpu.SMEM)
    outs = pl.pallas_call(
        functools.partial(block_kernel, z, tuple(scratch)),
        out_shape=(
            jax.ShapeDtypeStruct((images, z.share, width), bf16),
            jax.ShapeDtypeStruct((images, z.share, width), bf16),
            jax.ShapeDtypeStruct((z.re, 128), f32),
            jax.ShapeDtypeStruct((z.rl, 128), f32),
            jax.ShapeDtypeStruct((8, width), f32),
        ),
        in_specs=[hbm, smem, vmem, hbm, vmem, hbm, vmem, vmem, hbm, vmem, vmem, hbm, vmem, vmem, hbm],
        out_specs=(hbm, hbm, vmem, vmem, vmem),
        scratch_shapes=list(scratch.values()),
        compiler_params=pltpu.CompilerParams(
            collective_id=0, has_side_effects=True, vmem_limit_bytes=63 * 1024 * 1024
        ),
    )(
        tokens, image_count, token_place.reshape(1, -1), qkv_weight, bias_table, proj_weight,
        attention_gain.reshape(1, -1), attention_shift.reshape(1, -1), up_weight, hidden_gain.reshape(1, -1),
        hidden_shift.reshape(1, -1), down_weight, output_gain.reshape(1, -1), output_shift.reshape(1, -1), cotangent,
    )

    steps = 4
    block = pl.BlockSpec((images // steps, z.share, width), lambda i: (i, 0, 0))

    def whole(*shape):
        return jax.ShapeDtypeStruct(shape, f32), pl.BlockSpec(shape, lambda i: (0,) * len(shape))

    fh = z.F // H
    small = [
        whole(1, z.C, width), whole(1, length), whole(width // H, width), whole(1, width), whole(1, width),
        whole(width, fh), whole(1, fh), whole(1, fh), whole(fh, width), whole(1, width), whole(1, width)]
    big = jax.ShapeDtypeStruct((images, z.share, width), f32)
    res = pl.pallas_call(
        functools.partial(finish_kernel, z),
        grid=(steps,),
        out_shape=[big, big] + [a for a, _ in small],
        in_specs=[block, block, whole(z.re, 128)[1], whole(z.rl, 128)[1], whole(8, width)[1]],
        out_specs=[block, block] + [b for _, b in small],
    )(*outs)
    res = list(res)
    for k in (5, 6, 8, 9, 11, 12):
        res[k] = res[k].reshape(-1)
    return tuple(res)


def solution(mesh):
    H, B = mesh.shape["head"], mesh.shape["batch"]
    placed = (
        P("batch", None, None),
        P("batch"),
        P(),
        P("head", None, None),
        P("head", None),
        P(),
        P(),
        P(),
        P(None, "head"),
        P("head"),
        P("head"),
        P("head", None),
        P(),
        P(),
        P("batch", "head", None),
    )
    return jax.shard_map(
        functools.partial(on_device, H, B),
        mesh=mesh,
        in_specs=placed,
        out_specs=(
            P("batch", "head", None),
            P("batch", "head", None),
            P("head", None, None),
            P("head", None),
            P("head", None),
            P(),
            P(),
            P(None, "head"),
            P("head"),
            P("head"),
            P("head", None),
            P(),
            P(),
        ),
        check_vma=False,
    )
```

time: 878 us -> 164 us (0.19); the launches traced: 867 us -> 163 us
  waiting for transfers between devices: 335 us -> 0 us
  matrix products: 161 us -> 0 us
  blocking collectives: 158 us -> 0 us
  Pallas kernels: 0 us -> 147 us
  other arithmetic: 111 us -> 0 us
  local copies, waits for them, and re-layouts: 72.8 us -> 15.3 us
  between operations: 16.3 us -> 1.31 us
  starting transfers between devices: 11.6 us -> 0 us
    psum x2 -> x0, waiting for transfers between devices: 162 us -> none  [the longest x1 113 us: on_device(): lax.psum(grad_residual.astype(jnp.bfloat16), 'head').astype(jnp.float32)]
    dot_general x131 -> x0, matrix products: 161 us -> none  [the longest x1 23.2 us: on_device(): jnp.einsum('hk,tsk->hts', bias_table, onehot, precision=lax.Precision.HIG...]
    psum x7 -> x0, blocking collectives: 158 us -> none  [the longest x1 40.9 us: on_device(): lax.psum((jnp.sum(upstream, axis=(0, 1)), jnp.sum(upstream * normed_three...]
    pallas_call x0 -> x2, Pallas kernels: none -> 147 us  [the longest x1 142 us: on_device(): pl.pallas_call(functools.partial(block_kernel, z, tuple(scratch)), out_sh...]
    all_gather x2 -> x0, waiting for transfers between devices: 118 us -> none  [the longest x1 71 us: on_device(): lax.all_gather(active, 'head', axis=2, tiled=True)]
    convert_element_type x22 -> x0, other arithmetic: 57 us -> none  [the longest x12 13.5 us: attend_back(): grad_attended = (grad_act * silu_slope(attended)).astype(jnp.bfloat16)]
    unnamed x8 -> x0, waiting for transfers between devices: 55.3 us -> none
    add x16 -> x0, other arithmetic: 16.9 us -> none  [the longest x1 11 us: on_device(): tokens.astype(jnp.float32) + attention_gain * normed_one + attention_shift]
  transfers between devices with their start and end apart: 6 -> 0, of which waited for: 5 -> 0; matrix products, arithmetic and copies ran while one was open for 6% -> 0% of each run, Pallas kernels for 0% -> 0%
where the time goes in v1:
time: 164 us; the launch traced here: 163 us
  Pallas kernels  147 us (90%)
  local copies, waits for them, and re-layouts  15.3 us (9%)
    pallas_call x1, Pallas kernels, on_device(): pl.pallas_call(functools.partial(block_kernel, z, tuple(scratch)), out_sh...  142 us
    unnamed x6, local copies, waits for them, and re-layouts  15.3 us
    pallas_call x1, Pallas kernels, on_device(): pl.pallas_call(functools.partial(finish_kernel, z), grid=(steps,), out_sh...  5.1 us

profile of v1, /device:TPU:0, one launch (start us, length us, event | category | flops | bytes accessed | tf_op | source)
XLA Modules:
  0.0 163.3 jit_solution(11491010012565794036)
XLA Ops:
  1.3 2.8 %copy.29.refs_14_ = bf16[48,49,256]{2,1,0:T(8,128)(2,1)} copy(bf16[48,49,256]{2,0,1:T(8,128)(2,1)} %param.29) | data formatting | bytes 2408448 | tf_op args[14]
  4.1 6.3 %copy.28.refs_0_ = bf16[48,196,256]{2,1,0:T(8,128)(2,1)} copy(bf16[48,196,256]{2,0,1:T(8,128)(2,1)} %param.15) | data formatting | bytes 9633792 | tf_op args[0]
  10.3 141.6 %shard_map.246 = (bf16[48,49,256]{2,1,0:T(8,128)(2,1)}, bf16[48,49,256]{2,1,0:T(8,128)(2,1)}, f32[640,128]{1,0:T(8,128)}, f32[256,128]{1,0:T(8,128)}, f32[8,256]{1,0:T(8,128)}) custom-call(bf16[48,196,256]{2,1,0:T(8,128)(2,1)} %copy.28.refs_0_, s32[1]{0:T(128)S(6)} %copy.32.refs_1_, s32[1,196]{1,0:T(1,128)} %bitcast.13, f32[1,128,256]{2,1,0:T(8,128)} %refs_3_.1, ...), custom_call_target="tpu_custom_call" | custom-call | tf_op jit(solution)/shard_map/pallas_call | solution.py:639
  151.9 5.1 %shard_map.247 = (f32[48,49,256]{2,1,0:T(8,128)}, f32[48,49,256]{2,1,0:T(8,128)}, f32[1,128,256]{2,1,0:T(8,128)}, f32[1,196]{1,0:T(1,128)}, f32[64,256]{1,0:T(8,...) custom-call(bf16[48,49,256]{2,1,0:T(8,128)(2,1)} %get-tuple-element., ...), custom_call_target="tpu_custom_call" | custom-call | tf_op jit(solution)/shard_map/pallas_call | solution.py:671
  157.0 0.0 copy-start
  157.0 4.1 %copy.30 = f32[48,49,256]{2,0,1:T(8,128)} copy(f32[48,49,256]{2,1,0:T(8,128)} %get-tuple-element.49) | data formatting | bytes 4816896
  161.2 0.0 copy-done
  161.2 2.2 %copy.31 = f32[48,49,256]{2,0,1:T(8,128)} copy(f32[48,49,256]{2,1,0:T(8,128)S(1)} %copy-done) | data formatting | bytes 4816896
Async XLA Ops:
  157.0 4.1 %copy-start = (f32[48,49,256]{2,1,0:T(8,128)S(1)}, f32[48,49,256]{2,1,0:T(8,128)}, u32[]{:S(2)}) copy-start(f32[48,49,256]{2,1,0:T(8,128)} %get-tuple-element.50) | copy-start | bytes 7225348

commit v2 on v1

--- a/solution.py
+++ b/solution.py
@@ -66,16 +66,12 @@
     dma = pltpu.SemaphoreType.DMA
     vmem = pltpu.VMEM
     return {
-        "qkv32": vmem((C, D), f32),
-        "up32": vmem((D, F // H), f32),
-        "down32": vmem((F // H, D), f32),
-        "proj32": vmem((D, D), f32),
-        "xraw": vmem((n, z.length, D), bf16),
+        "xt": vmem((T, 16, D), bf16),
+        "ct": vmem((T, 16, D), bf16),
+        "mix": vmem((n * 16, 256), bf16),
         "qkvg": vmem((H, C, D), bf16),
-        "upg": vmem((H, D, F // H), bf16),
         "downg": vmem((H, F // H, D), bf16),
         "smallg": vmem((H, 4, 128), f32),
-        "ct": vmem((H, n, z.share, D), bf16),
         "w2": vmem((H * C, D), bf16),
         "w2t": vmem((D, H * C), bf16),
         "upcat": vmem((D, F), bf16),
@@ -105,24 +101,16 @@
         "gproj": vmem((n, L, D), bf16),
         "tmp": vmem((T, D), f32),
         "osend": vmem((H, n, z.share, D), bf16),
+        "tsend": vmem((H, n, z.share, D), bf16),
         "dmt": vmem((H * C, L), bf16),
         "gdown": vmem((D, F), f32),
         "gup": vmem((D, F), f32),
         "gpr": vmem((D, D), f32),
         "gqkv": vmem((H * C, D), f32),
         "srow": vmem((2, F), f32),
-        "ar0h": vmem((H, 4, D), f32),
-        "ar0b": vmem((B, 4, D), f32),
-        "ar1h": vmem((H, 2, F), f32),
-        "ar1b": vmem((B, 2, F), f32),
-        "ar2h": vmem((H, 4, D), f32),
-        "ar2b": vmem((B, 4, D), f32),
-        "ar3h": vmem((H, 2, F), f32),
-        "ar3b": vmem((B, 2, F), f32),
-        "ar4h": vmem((H, 2, D), f32),
-        "ar4b": vmem((B, 2, D), f32),
-        "ar5h": vmem((H, H, L), f32),
-        "ar5b": vmem((B, H, L), f32),
+        "brow": vmem((H, 1, L), f32),
+        **z.sums,
+        "cnt": vmem((B, 1, 128), f32),
         "ge1": vmem((H, z.re, 128), bf16),
         "ge1r": vmem((H, z.re, 128), bf16),
         "ge2": vmem((B, z.re // B, 128), f32),
@@ -136,10 +124,10 @@
         "loc": dma((8,)),
         "hs": dma((9, H)),
         "hr": dma((9, H)),
-        "ahs": dma((6, H)),
-        "ahr": dma((6, H)),
-        "abs": dma((6, B)),
-        "abr": dma((6, B)),
+        "ass": dma((6, z.ports)),
+        "asr": dma((6, z.ports)),
+        "cns": dma((B,)),
+        "cnr": dma((B,)),
         "gbs": dma((4, B)),
         "gbr": dma((4, B)),
     }
@@ -176,40 +164,71 @@
         else:
             lax.fori_loop(1, size, lambda j, c: (step(j), c)[1], 0)
 
-    c_qkv = local(qkv_w.at[0], s.qkv32, 0)
-    c_up = local(up_w, s.up32, 1)
-    c_down = local(down_w, s.down32, 2)
-    c_tok = local(tokens.at[pl.ds(me_h * n, n)], s.xraw, 3)
-    c_proj = local(proj_w, s.proj32, 4)
+    FH = F // H
+    PH = D // H
+    own = pl.ds(pl.multiple_of(me_h * FH, FH), FH)
+    qkv_32, up_32, down_32 = s.gqkv.at[0:C], s.gup.at[:, 0:FH], s.gdown.at[0:FH, 0:D]
+    c_qkv = local(qkv_w.at[0], qkv_32, 0)
+    c_up = local(up_w, up_32, 1)
+    c_down = local(down_w, down_32, 2)
+    def window(slot):
+        return pl.multiple_of(slot * n // 8 * 8, 8)
+
+    c_tok = local(tokens.at[:, pl.ds(window(me_h), 16)], s.xt.at[pl.ds(0, length)], 3)
+    c_proj = local(proj_w, s.gpr, 4)
+
+    def everyone():
+        pairs = [(a, b) for a in range(H) for b in range(B) if a or b]
+        return sorted(pairs, key=lambda p: -(p[0] % 2 + p[0] // 2 + (2 if p[1] > 1 else p[1] / 4)))
+
+    def at_offset(offset):
+        a, b = offset
+        x, y = lax.rem(me_h, 2), lax.div(me_h, 2)
+        other = (y + a // 2 - 2 * y * (a // 2)) * 2 + x + a % 2 - 2 * x * (a % 2)
+        return {"head": other, "batch": lax.rem(me_b + b, B)}
 
     barrier = pltpu.get_barrier_semaphore()
-    around(H, lambda j: pl.semaphore_signal(
-        barrier, inc=1, device_id={"head": lax.rem(me_h + j, H)}, device_id_type=MESH))
-    around(B, lambda j: pl.semaphore_signal(
-        barrier, inc=1, device_id={"batch": lax.rem(me_b + j, B)}, device_id_type=MESH))
+    if z.direct:
+        for offset in everyone():
+            pl.semaphore_signal(barrier, inc=1, device_id=at_offset(offset), device_id_type=MESH)
+    else:
+        around(H, lambda j: pl.semaphore_signal(
+            barrier, inc=1, device_id={"head": lax.rem(me_h + j, H)}, device_id_type=MESH))
+        around(B, lambda j: pl.semaphore_signal(
+            barrier, inc=1, device_id={"batch": lax.rem(me_b + j, B)}, device_id_type=MESH))
 
     s.smallg[me_h] = jnp.concatenate(
         [gain_2[...], shift_2[...], table[:, 0:128], jnp.concatenate(
             [table[:, 128:length], jnp.zeros((1, 256 - length), f32)], axis=1)], axis=0)
     c_qkv.wait()
-    s.qkvg[me_h] = s.qkv32[...].astype(bf16)
+    s.qkvg[me_h] = qkv_32[...].astype(bf16)
     c_up.wait()
-    s.upg[me_h] = s.up32[...].astype(bf16)
+    s.upcat[:, own] = up_32[...].astype(bf16)
     c_down.wait()
-    s.downg[me_h] = s.down32[...].astype(bf16)
-
-    pl.semaphore_wait(barrier, H - 1 + B - 1)
-
-    weights = (s.qkvg, s.smallg, s.upg, s.downg)
-    for k in range(2):
+    s.downg[me_h] = down_32[...].astype(bf16)
+
+    s.cnt[me_b] = jnp.full((1, 128), count[0]).astype(f32)
+    pl.semaphore_wait(barrier, H * B - 1 if z.direct else H - 1 + B - 1)
+
+    shared = (s.qkvg.at[me_h], s.smallg.at[me_h], s.upcat.at[:, own], s.downg.at[me_h])
+
+    def weight_copy(k, j):
+        return to_head(shared[k], shared[k], k, j)
+
+    for k in range(4):
         for j in range(1, H):
-            to_head(weights[k].at[me_h], weights[k].at[me_h], k, j).start()
-    for k in range(2, 4):
-        for j in range(1, H):
-            to_head(weights[k].at[me_h], weights[k].at[me_h], k, j).start()
+            weight_copy(k, j).start()
+    def cot_copy(j):
+        peer = lax.rem(me_h + j, H)
+        return to_head(cot.at[:, pl.ds(window(peer), 16)], s.ct.at[pl.ds(me_h * share, share)], 4, j)
+
+    def count_copy(j):
+        return to_batch(s.cnt.at[me_b], s.cnt.at[me_b], s.cns.at[j], s.cnr.at[j], j)
+
+    around(B, lambda j: count_copy(j).start())
     for j in range(1, H):
-        to_head(cot.at[pl.ds(lax.rem(me_h + j, H) * n, n)], s.ct.at[me_h], 4, j).start()
-    c_cot = local(cot.at[pl.ds(me_h * n, n)], s.ct.at[me_h], 5)
+        cot_copy(j).start()
+    c_cot = local(cot.at[:, pl.ds(window(me_h), 16)], s.ct.at[pl.ds(me_h * share, share)], 5)
 
     row_at = lax.broadcasted_iota(jnp.int32, (L, L), 0)
     lane_at = lax.broadcasted_iota(jnp.int32, (L, L), 1)
@@ -236,27 +255,43 @@
     s.dmt[...] = jnp.zeros(s.dmt.shape, bf16)
     s.gdown[...] = jnp.zeros(s.gdown.shape, f32)
     s.gup[...] = jnp.zeros(s.gup.shape, f32)
-    s.gpr[...] = jnp.zeros(s.gpr.shape, f32)
     s.gqkv[...] = jnp.zeros(s.gqkv.shape, f32)
 
     def valid_of(i):
         return jnp.where(me_h * n + i < count[0], 1.0, 0.0)
 
     c_proj.wait()
-    s.projw[...] = s.proj32[...].astype(bf16)
+    s.projw[...] = s.gpr[...].astype(bf16)
+    s.gpr[...] = jnp.zeros(s.gpr.shape, f32)
+    line_at = lax.broadcasted_iota(jnp.int32, (n * 16, 256), 0)
+    pick_at = lax.broadcasted_iota(jnp.int32, (n * 16, 256), 1)
+    image_at = lax.shift_right_logical(line_at, 4)
+    s.mix[...] = jnp.where(
+        (lax.bitwise_and(line_at, 15) == lax.shift_right_logical(pick_at, 4))
+        & (lax.bitwise_and(pick_at, 15) == image_at + (me_h * n - window(me_h)))
+        & (image_at + me_h * n < count[0]),
+        1.0, 0.0).astype(bf16)
+    s.xt[length:T] = jnp.zeros((T - length, 16, D), bf16)
+    s.ct[length:T] = jnp.zeros((T - length, 16, D), bf16)
+    s.xpad[:, T:L, :] = jnp.zeros((n, L - T, D), bf16)
+    s.gproj[:, T:L, :] = jnp.zeros((n, L - T, D), bf16)
     c_tok.wait()
 
-    def pad(i, carry):
-        s.xpad[i] = jnp.zeros((L, D), bf16)
-        s.xpad[i, 0:length, :] = (s.xraw[i].astype(f32) * valid_of(i)).astype(bf16)
-        s.gproj[i, T:L, :] = jnp.zeros((L - T, D), bf16)
+    def enter_tokens(k, carry):
+        at = pl.ds(pl.multiple_of(k * 16, 16), 16)
+        s.xpad[:, at, :] = nn(s.mix[...], s.xt[at].reshape(256, D)).astype(bf16).reshape(n, 16, D)
         return carry
 
-    lax.fori_loop(0, n, pad, 0)
+    def enter_cotangent(k, carry):
+        at = pl.ds(pl.multiple_of(k * 16, 16), 16)
+        s.u[:, at, :] = nn(s.mix[...], s.ct[at].reshape(256, D)).reshape(n, 16, D)
+        return carry
+
+    lax.fori_loop(0, T // 16, enter_tokens, 0)
 
     for k in range(2):
         for j in range(1, H):
-            to_head(weights[k].at[me_h], weights[k].at[me_h], k, j).wait()
+            weight_copy(k, j).wait()
     for h in range(H):
         s.w2[h * KEY : (h + 1) * KEY] = s.qkvg[h, 0:KEY]
         s.w2[(H + h) * KEY : (H + h + 1) * KEY] = s.qkvg[h, KEY : 2 * KEY]
@@ -297,51 +332,82 @@
     def zeros(width):
         return jnp.zeros((8, width), f32)
 
-    def all_reduce(k, rows, hbuf, bbuf):
-        for r, row in enumerate(rows):
-            hbuf[me_h, r : r + 1, :] = row
+    def port(k, src, slot, offset, j):
+        return pltpu.make_async_remote_copy(
+            src_ref=src, dst_ref=slot, send_sem=s.ass.at[k, j], recv_sem=s.asr.at[k, j],
+            device_id=offset, device_id_type=MESH)
+
+    def sum_slots(buf, size):
+        if size <= 32:
+            whole = buf[0]
+            for b in range(1, size):
+                whole = whole + buf[b]
+            return whole
+        return lax.fori_loop(1, size, lambda b, c: c + buf[b], buf[0])
+
+    def sum_copies(k):
+        buf = z.bufs(s, k)[0]
+        if z.direct:
+            me = me_h * B + me_b
+            return [port(k, buf.at[me], buf.at[me], at_offset(o), j) for j, o in enumerate(everyone())]
+        return [port(k, buf.at[me_h], buf.at[me_h], {"head": lax.rem(me_h + j, H)}, j) for j in range(1, H)]
+
+    def start_sum(k, rows):
+        buf = z.bufs(s, k)[0]
+        me = me_h * B + me_b if z.direct else me_h
+        r = 0
+        for row in rows:
+            for c in range(row.shape[1] // 128):
+                buf[me, r : r + 1, :] = row[:, c * 128 : (c + 1) * 128]
+                r += 1
+        for copy in sum_copies(k):
+            copy.start()
+
+    def finish_sum(k, width):
+        for copy in sum_copies(k):
+            copy.wait()
+        bufs = z.bufs(s, k)
+        if z.direct:
+            whole = sum_slots(bufs[0], H * B)
+        else:
+            bufs[1][me_b] = sum_slots(bufs[0], H)
+            around(B, lambda j: port(
+                k, bufs[1].at[me_b], bufs[1].at[me_b], {"batch": lax.rem(me_b + j, B)}, H + j).start())
+            around(B, lambda j: port(
+                k, bufs[1].at[me_b], bufs[1].at[me_b], {"batch": lax.rem(me_b + j, B)}, H + j).wait())
+            whole = sum_slots(bufs[1], B)
+        step = width // 128
+        return [
+            jnp.concatenate([whole[r + c : r + c + 1] for c in range(step)], axis=1)
+            for r in range(0, whole.shape[0], step)
+        ]
+
+    first, second = lax.fori_loop(0, n, attend, (zeros(D), zeros(D)))
+    start_sum(0, [total(first), total(second)])
+    for j in range(1, H):
+        cot_copy(j).wait()
+    c_cot.wait()
+    lax.fori_loop(0, T // 16, enter_cotangent, 0)
+    for k in range(2, 4):
         for j in range(1, H):
-            pltpu.make_async_remote_copy(
-                src_ref=hbuf.at[me_h], dst_ref=hbuf.at[me_h], send_sem=s.ahs.at[k, j], recv_sem=s.ahr.at[k, j],
-                device_id={"head": lax.rem(me_h + j, H)}, device_id_type=MESH).start()
-        for j in range(1, H):
-            pltpu.make_async_remote_copy(
-                src_ref=hbuf.at[me_h], dst_ref=hbuf.at[me_h], send_sem=s.ahs.at[k, j], recv_sem=s.ahr.at[k, j],
-                device_id={"head": lax.rem(me_h + j, H)}, device_id_type=MESH).wait()
-        part = hbuf[0]
-        for h in range(1, H):
-            part = part + hbuf[h]
-        bbuf[me_b] = part
-        around(B, lambda j: to_batch(bbuf.at[me_b], bbuf.at[me_b], s.abs.at[k, j], s.abr.at[k, j], j).start())
-        around(B, lambda j: to_batch(bbuf.at[me_b], bbuf.at[me_b], s.abs.at[k, j], s.abr.at[k, j], j).wait())
-        if B <= 8:
-            whole = bbuf[0]
-            for b in range(1, B):
-                whole = whole + bbuf[b]
-            return whole
-        return lax.fori_loop(1, B, lambda b, c: c + bbuf[b], bbuf[0])
-
-    first, second = lax.fori_loop(0, n, attend, (zeros(D), zeros(D)))
-    mine = jnp.clip(count[0] - me_h * n, 0, n).astype(f32) * float(length)
-    sums = all_reduce(
-        0, [total(first), total(second), jnp.full((1, D), mine), jnp.zeros((1, D), f32)], s.ar0h, s.ar0b)
-    seen_row = sums[2:3, :]
+            weight_copy(k, j).wait()
+    down = s.downg[...].reshape(F, D)
+    s.w2t[...] = nt(s.eye[...], s.w2[...]).astype(bf16)
+    gain_2w = jnp.concatenate([s.smallg[h, 0:1, :] for h in range(H)], axis=1)
+    shift_2w = jnp.concatenate([s.smallg[h, 1:2, :] for h in range(H)], axis=1)
+    around(B, lambda j: count_copy(j).wait())
+    seen_part = sum_slots(s.cnt, B) * float(length)
+    seen_row = jnp.concatenate([seen_part] * (D // 128), axis=1)
+    sums = finish_sum(0, D)
     seen_wide = jnp.concatenate([seen_row] * (F // D), axis=1)
 
     def moments(first, second, seen):
         mean = first / seen
         return mean, lax.rsqrt(second / seen - mean * mean + EPSILON)
 
-    mean_1, inverse_1 = moments(sums[0:1], sums[1:2], seen_row)
+    mean_1, inverse_1 = moments(sums[0], sums[1], seen_row)
     a_1 = gain_1[...] * inverse_1
     b_1 = shift_1[...] - mean_1 * a_1
-
-    for k in range(2, 4):
-        for j in range(1, H):
-            to_head(weights[k].at[me_h], weights[k].at[me_h], k, j).wait()
-    for h in range(H):
-        s.upcat[:, h * (F // H) : (h + 1) * (F // H)] = s.upg[h]
-    down = s.downg[...].reshape(F, D)
 
     def residual_of(i):
         return s.xpad[i, 0:T].astype(f32) + (s.proj[i] * a_1 + (b_1 * valid_of(i)) * s.rowmask[...])
@@ -355,16 +421,11 @@
         return first + fold(hidden), second + fold(hidden * hidden)
 
     first, second = lax.fori_loop(0, n, enter, (zeros(F), zeros(F)))
-    sums = all_reduce(1, [total(first), total(second)], s.ar1h, s.ar1b)
-    mean_2, inverse_2 = moments(sums[0:1], sums[1:2], seen_wide)
-    gain_2w = jnp.concatenate([s.smallg[h, 0:1, :] for h in range(H)], axis=1)
-    shift_2w = jnp.concatenate([s.smallg[h, 1:2, :] for h in range(H)], axis=1)
+    start_sum(1, [total(first), total(second)])
+    sums = finish_sum(1, F)
+    mean_2, inverse_2 = moments(sums[0], sums[1], seen_wide)
     a_2 = gain_2w * inverse_2
     b_2 = shift_2w - mean_2 * a_2
-
-    for j in range(1, H):
-        to_head(cot.at[pl.ds(lax.rem(me_h + j, H) * n, n)], s.ct.at[me_h], 4, j).wait()
-    c_cot.wait()
 
     def leave(i, carry):
         one, two, three, four = carry
@@ -377,21 +438,19 @@
         outgoing = nn(low, down)
         s.out[i] = outgoing
         valid = valid_of(i)
-        s.u[i, T - 16 : T, :] = jnp.zeros((16, D), f32)
-        for q in range(H):
-            s.u[i, q * share : (q + 1) * share, :] = s.ct[q, i].astype(f32) * valid
         upstream = s.u[i]
         masked = outgoing * (s.rowmask[...] * valid)
         return (one + fold(masked), two + fold(masked * outgoing), three + fold(upstream),
                 four + fold(upstream * outgoing))
 
     sums = lax.fori_loop(0, n, leave, (zeros(D), zeros(D), zeros(D), zeros(D)))
-    sums = all_reduce(2, [total(v) for v in sums], s.ar2h, s.ar2b)
-    mean_3, inverse_3 = moments(sums[0:1], sums[1:2], seen_row)
+    start_sum(2, [total(v) for v in sums])
+    sums = finish_sum(2, D)
+    mean_3, inverse_3 = moments(sums[0], sums[1], seen_row)
     a_3 = gain_3[...] * inverse_3
     b_3 = shift_3[...] - mean_3 * a_3
-    sum_shift_3 = sums[2:3]
-    sum_gain_3 = inverse_3 * (sums[3:4] - mean_3 * sum_shift_3)
+    sum_shift_3 = sums[2]
+    sum_gain_3 = inverse_3 * (sums[3] - mean_3 * sum_shift_3)
 
     def back(gain, mean, inverse, sum_shift, sum_gain, seen):
         scaled = gain * inverse
@@ -402,27 +461,28 @@
 
     def back_leave(i, carry):
         one, two = carry
-        valid = valid_of(i)
-        outgoing = s.out[i]
-        s.tmp[...] = (residual_of(i) + (outgoing * a_3 + b_3)) * valid
+        mask = s.rowmask[...] * valid_of(i)
+        grad = (s.u[i] * s_3 + (s.out[i] * v_3 + r_3) * mask).astype(bf16)
+        s.gproj[i, 0:T, :] = grad
+        shaped = nt(grad, down) * s.slope[i]
+        s.slope[i] = shaped
+        return one + fold(shaped), two + fold(shaped * s.hid[i])
+
+    def down_gradient(i, carry):
+        turned = nt(s.eye[...], s.gproj[i, 0:T, :]).astype(bf16)
+        s.gdown[...] += nn(turned, s.act2[i])
+        s.tmp[...] = (residual_of(i) + (s.out[i] * a_3 + b_3)) * valid_of(i)
         for q in range(H):
             s.osend[q, i] = s.tmp[q * share : (q + 1) * share, :].astype(bf16)
-        grad = (s.u[i] * s_3 + (outgoing * v_3 + r_3) * (s.rowmask[...] * valid)).astype(bf16)
-        shaped = nt(grad, down) * s.slope[i]
-        s.slope[i] = shaped
-        turned = nt(s.eye[...], grad).astype(bf16)
-        s.gdown[...] += nn(turned, s.act2[i])
-        return one + fold(shaped), two + fold(shaped * s.hid[i])
+        return carry
 
     first, second = lax.fori_loop(0, n, back_leave, (zeros(F), zeros(F)))
-    sums = all_reduce(3, [total(first), total(second)], s.ar3h, s.ar3b)
-
-    for j in range(1, H):
-        to_head(s.osend.at[lax.rem(me_h + j, H)], out_o.at[pl.ds(me_h * n, n)], 5, j).start()
-    c_out = local(s.osend.at[me_h], out_o.at[pl.ds(me_h * n, n)], 6)
-
-    sum_shift_2 = sums[0:1]
-    sum_gain_2 = inverse_2 * (sums[1:2] - mean_2 * sum_shift_2)
+    start_sum(3, [total(first), total(second)])
+    lax.fori_loop(0, n, down_gradient, 0)
+    sums = finish_sum(3, F)
+
+    sum_shift_2 = sums[0]
+    sum_gain_2 = inverse_2 * (sums[1] - mean_2 * sum_shift_2)
     s_2, v_2, r_2 = back(gain_2w, mean_2, inverse_2, sum_shift_2, sum_gain_2, seen_wide)
     s.srow[0:1, :] = sum_gain_2
     s.srow[1:2, :] = sum_shift_2
@@ -431,16 +491,26 @@
         one, two = carry
         mask = s.rowmask[...] * valid_of(i)
         grad = (s.slope[i] * s_2 + s.hid[i] * v_2 + r_2 * jnp.concatenate([mask] * (F // D), axis=1)).astype(bf16)
-        turned = nt(s.eye[...], s.res[i]).astype(bf16)
-        s.gup[...] += nn(turned, grad)
+        s.act2[i] = grad
         upstream = s.u[i] + nt(grad, s.upcat[...])
         s.u[i] = upstream
         return one + fold(upstream), two + fold(upstream * s.proj[i])
 
     first, second = lax.fori_loop(0, n, back_enter, (zeros(D), zeros(D)))
-    sums = all_reduce(4, [total(first), total(second)], s.ar4h, s.ar4b)
-    sum_shift_1 = sums[0:1]
-    sum_gain_1 = inverse_1 * (sums[1:2] - mean_1 * sum_shift_1)
+    start_sum(4, [total(first), total(second)])
+
+    def up_gradient(i, carry):
+        turned = nt(s.eye[...], s.res[i]).astype(bf16)
+        s.gup[...] += nn(turned, s.act2[i])
+        return carry
+
+    lax.fori_loop(0, n, up_gradient, 0)
+    sums = finish_sum(4, D)
+    for j in range(1, H):
+        to_head(s.osend.at[lax.rem(me_h + j, H)], out_o.at[pl.ds(me_h * n, n)], 5, j).start()
+    c_out = local(s.osend.at[me_h], out_o.at[pl.ds(me_h * n, n)], 6)
+    sum_shift_1 = sums[0]
+    sum_gain_1 = inverse_1 * (sums[1] - mean_1 * sum_shift_1)
     s_1, v_1, r_1 = back(gain_1[...], mean_1, inverse_1, sum_shift_1, sum_gain_1, seen_row)
 
     def back_project(i, carry):
@@ -473,8 +543,6 @@
             return whole
         return lax.fori_loop(1, B, lambda j, c: c + received[lax.rem(me_b + j, B)], own)
 
-    FH = F // H
-    PH = D // H
     for h in range(H):
         s.ge1[h, 0:D, :] = s.gup[:, h * FH : (h + 1) * FH].astype(bf16)
         s.ge1[h, D : 2 * D, :] = s.gdown[:, h * FH : (h + 1) * FH].astype(bf16)
@@ -485,10 +553,6 @@
             s.ge1[h, 2 * D + PH * (D // 128) :, :] = jnp.zeros((z.re - 2 * D - PH * (D // 128), 128), bf16)
     for copy in shares((s.ge1, s.ge1r), 7):
         copy.start()
-
-    for j in range(1, H):
-        to_head(s.osend.at[lax.rem(me_h + j, H)], out_o.at[pl.ds(me_h * n, n)], 5, j).wait()
-    c_out.wait()
 
     def back_attend(i, carry):
         slope_gate = sigmoid(s.att[i])
@@ -515,13 +579,12 @@
         turned = nn(s.w2t[...], s.dmt[...]).astype(bf16)
         s.tmp[...] = s.u[i] + nt(s.eyet[...], turned)
         for q in range(H):
-            s.osend[q, i] = s.tmp[q * share : (q + 1) * share, :].astype(bf16)
+            s.tsend[q, i] = s.tmp[q * share : (q + 1) * share, :].astype(bf16)
         for j in range(1, H):
-            to_head(s.osend.at[lax.rem(me_h + j, H), i], tg_o.at[me_h * n + i], 6, j).start()
-        pltpu.make_async_copy(s.osend.at[me_h, i], tg_o.at[me_h * n + i], s.loc.at[7]).start()
+            to_head(s.tsend.at[lax.rem(me_h + j, H), i], tg_o.at[me_h * n + i], 6, j).start()
+        pltpu.make_async_copy(s.tsend.at[me_h, i], tg_o.at[me_h * n + i], s.loc.at[7]).start()
         return carry
 
-    s.w2t[...] = nt(s.eye[...], s.w2[...]).astype(bf16)
     lax.fori_loop(0, n // 2, back_attend, 0)
 
     for copy in shares((s.ge1, s.ge1r), 7):
@@ -570,18 +633,18 @@
         for index, good in picks:
             line = line + jnp.where(good, take(ordered[:, 0:128], ordered[:, 128:256], index), 0.0)
         bias_rows.append(total(line * s.rowmask[...]))
-    bias_sums = all_reduce(5, bias_rows, s.ar5h, s.ar5b)
-    s.ar5h[0] = bias_sums
+    start_sum(5, bias_rows)
 
     for copy in shares((s.gl1, s.gl1r), 8):
         copy.wait()
     s.gl2[...] = head_sum((s.gl1, s.gl1r)).reshape(B, z.rl // B, 128)
     spread(lambda peer: s.gl2.at[peer], s.gl2r.at[me_b], 2, lambda c: c.start())
+    for h, row in enumerate(finish_sum(5, L)):
+        s.brow[h] = row
     spread(lambda peer: s.gl2.at[peer], s.gl2r.at[me_b], 2, lambda c: c.wait())
     s.gl3[me_b] = batch_sum(s.gl2[me_b], s.gl2r)
     spread(lambda peer: s.gl3.at[me_b], s.gl3.at[me_b], 3, lambda c: c.start())
 
-    own = pl.ds(pl.multiple_of(me_h * FH, FH), FH)
     small_o[...] = jnp.zeros(small_o.shape, f32)
     small_o[0:1, :] = sum_gain_1
     small_o[1:2, :] = sum_shift_1
@@ -589,7 +652,7 @@
     small_o[3:4, :] = sum_shift_3
     small_o[4:5, 0:FH] = s.srow[0:1, own]
     small_o[5:6, 0:FH] = s.srow[1:2, own]
-    small_o[6:7, :] = s.ar5h[0, pl.ds(me_h, 1), :]
+    small_o[6:7, :] = s.brow[me_h]
 
     spread(lambda peer: s.ge3.at[me_b], s.ge3.at[me_b], 1, lambda c: c.wait())
     early_o[...] = s.ge3[...].reshape(z.re, 128)
@@ -597,13 +660,22 @@
     late_o[...] = s.gl3[...].reshape(z.rl, 128)
 
     for j in range(1, H):
-        to_head(s.osend.at[lax.rem(me_h + j, H)], tg_o.at[pl.ds(me_h * n, n)], 6, j).wait()
-    pltpu.make_async_copy(s.osend.at[me_h], tg_o.at[pl.ds(me_h * n, n)], s.loc.at[7]).wait()
+        to_head(s.osend.at[lax.rem(me_h + j, H)], out_o.at[pl.ds(me_h * n, n)], 5, j).wait()
+        to_head(s.tsend.at[lax.rem(me_h + j, H)], tg_o.at[pl.ds(me_h * n, n)], 6, j).wait()
+    c_out.wait()
+    pltpu.make_async_copy(s.tsend.at[me_h], tg_o.at[pl.ds(me_h * n, n)], s.loc.at[7]).wait()
 
 
 def finish_kernel(z, out_i, tg_i, early, late, small, out, tg, qkv, bias, proj, g1, s1, up, g2, s2, down, g3, s3):
-    out[...] = out_i[...].astype(f32)
-    tg[...] = tg_i[...].astype(f32)
+    at = lax.broadcasted_iota(jnp.int32, (128, 128), 0)
+    to = lax.broadcasted_iota(jnp.int32, (128, 128), 1)
+    turn = jnp.where(lax.bitwise_and(at, 7) * 16 + lax.shift_right_logical(at, 3) == to, 1.0, 0.0).astype(bf16)
+    for src, dst in ((out_i, out), (tg_i, tg)):
+        rows = z.share // 16 * 16
+        for k in range(0, rows, 16):
+            dst[k : k + 16] = nn(turn, src[:, k : k + 16, :].reshape(128, z.D)).reshape(16, 8, z.D)
+        for k in range(rows, z.share):
+            dst[k] = src[:, k, :].astype(f32)
 
     @pl.when(pl.program_id(0) == 0)
     def _():
@@ -632,6 +704,19 @@
         H=H, B=B, C=qkv_weight.shape[1], share=cotangent.shape[1], length=length)
     z.re = round_up(2 * z.D + z.D // H * (z.D // 128), 8 * max(B, 2))
     z.rl = round_up(z.C * (z.D // 128), 8 * max(B, 2))
+    z.direct = H == 4 and B <= 8
+    z.ports = H * B if z.direct else H + B
+    z.sums = {}
+    for k, r in enumerate((2 * z.D, 2 * z.F, 4 * z.D, 2 * z.F, 2 * z.D, H * z.L)):
+        z.sums["sum%d" % k] = pltpu.VMEM((H * B if z.direct else H, r // 128, 128), f32)
+        if not z.direct:
+            z.sums["part%d" % (k % 2)] = pltpu.VMEM((B, 8, 128), f32)
+
+    def bufs(s, k):
+        first = getattr(s, "sum%d" % k)
+        return first, None if z.direct else getattr(s, "part%d" % (k % 2)).at[:, 0 : first.shape[1]]
+
+    z.bufs = bufs
     scratch = layout(z)
     hbm = pl.BlockSpec(memory_space=pl.ANY)
     vmem = pl.BlockSpec(memory_space=pltpu.VMEM)
@@ -649,16 +734,18 @@
         out_specs=(hbm, hbm, vmem, vmem, vmem),
         scratch_shapes=list(scratch.values()),
         compiler_params=pltpu.CompilerParams(
-            collective_id=0, has_side_effects=True, vmem_limit_bytes=63 * 1024 * 1024
+            collective_id=0, has_side_effects=True, vmem_limit_bytes=127 * 512 * 1024
         ),
     )(
-        tokens, image_count, token_place.reshape(1, -1), qkv_weight, bias_table, proj_weight,
+        tokens.transpose(1, 0, 2), image_count, token_place.reshape(1, -1), qkv_weight, bias_table, proj_weight,
         attention_gain.reshape(1, -1), attention_shift.reshape(1, -1), up_weight, hidden_gain.reshape(1, -1),
-        hidden_shift.reshape(1, -1), down_weight, output_gain.reshape(1, -1), output_shift.reshape(1, -1), cotangent,
+        hidden_shift.reshape(1, -1), down_weight, output_gain.reshape(1, -1), output_shift.reshape(1, -1),
+        cotangent.transpose(1, 0, 2),
     )
 
-    steps = 4
-    block = pl.BlockSpec((images // steps, z.share, width), lambda i: (i, 0, 0))
+    steps = images // 8
+    block = pl.BlockSpec((8, z.share, width), lambda i: (i, 0, 0))
+    turned = pl.BlockSpec((z.share, 8, width), lambda i: (0, i, 0))
 
     def whole(*shape):
         return jax.ShapeDtypeStruct(shape, f32), pl.BlockSpec(shape, lambda i: (0,) * len(shape))
@@ -667,15 +754,15 @@
     small = [
         whole(1, z.C, width), whole(1, length), whole(width // H, width), whole(1, width), whole(1, width),
         whole(width, fh), whole(1, fh), whole(1, fh), whole(fh, width), whole(1, width), whole(1, width)]
-    big = jax.ShapeDtypeStruct((images, z.share, width), f32)
+    big = jax.ShapeDtypeStruct((z.share, images, width), f32)
     res = pl.pallas_call(
         functools.partial(finish_kernel, z),
         grid=(steps,),
         out_shape=[big, big] + [a for a, _ in small],
         in_specs=[block, block, whole(z.re, 128)[1], whole(z.rl, 128)[1], whole(8, width)[1]],
-        out_specs=[block, block] + [b for _, b in small],
+        out_specs=[turned, turned] + [b for _, b in small],
     )(*outs)
-    res = list(res)
+    res = [res[0].transpose(1, 0, 2), res[1].transpose(1, 0, 2), *res[2:]]
     for k in (5, 6, 8, 9, 11, 12):
         res[k] = res[k].reshape(-1)
     return tuple(res)

time: 164 us -> 140 us (0.85)
  local copies, waits for them, and re-layouts: 15.3 us -> 0 us
  Pallas kernels: 147 us -> 138 us
    unnamed x6 -> x0, local copies, waits for them, and re-layouts: 15.3 us -> none
    pallas_call x1, Pallas kernels: 142 us -> 131 us  [on_device(): pl.pallas_call(functools.partial(block_kernel, z, tuple(scratch)), out_sh...]
    pallas_call x1, Pallas kernels: 5.1 us -> 6.83 us  [on_device(): pl.pallas_call(functools.partial(finish_kernel, z), grid=(steps,), out_sh...]
where the time goes in v2:
time: 140 us
  Pallas kernels  138 us (99%)
  between operations  1.46 us (1%)
    pallas_call x1, Pallas kernels, on_device(): pl.pallas_call(functools.partial(block_kernel, z, tuple(scratch)), out_sh...  131 us
    pallas_call x1, Pallas kernels, on_device(): pl.pallas_call(functools.partial(finish_kernel, z), grid=(steps,), out_sh...  6.83 us

profile of v2, /device:TPU:0, one launch (start us, length us, event | category | flops | bytes accessed | tf_op | source)
XLA Modules:
  0.0 139.6 jit_solution(12204871020259487408)
XLA Ops:
  1.3 131.3 %shard_map.246 = (bf16[48,49,256]{2,1,0:T(8,128)(2,1)}, bf16[48,49,256]{2,1,0:T(8,128)(2,1)}, f32[640,128]{1,0:T(8,128)}, f32[256,128]{1,0:T(8,128)}, f32[8,256]{1,0:T(8,128)}) custom-call(bf16[196,48,256]{2,1,0:T(8,128)(2,1)} %bitcast.17, s32[1]{0:T(128)S(6)} %copy.28.refs_1_, s32[1,196]{1,0:T(1,128)} %bitcast.19, f32[1,128,256]{2,1,0:T(8,128)} %refs_3_.1, ...), custom_call_target="tpu_custom_call" | custom-call | tf_op jit(solution)/shard_map/pallas_call | solution.py:724
  132.6 6.8 %shard_map.247 = (f32[49,48,256]{2,1,0:T(8,128)}, f32[49,48,256]{2,1,0:T(8,128)}, f32[1,128,256]{2,1,0:T(8,128)}, f32[1,196]{1,0:T(1,128)}, f32[64,256]{1,0:T(8,...) custom-call(bf16[48,49,256]{2,1,0:T(8,128)(2,1)} %get-tuple-element., ...), custom_call_target="tpu_custom_call" | custom-call | tf_op jit(solution)/shard_map/pallas_call | solution.py:758

commit v3 on v2

--- a/solution.py
+++ b/solution.py
@@ -24,6 +24,29 @@
 
 def nt(left, right):
     return lax.dot_general(left, right, (((1,), (1,)), ((), ())), preferred_element_type=f32)
+
+
+def tn(left, right):
+    return lax.dot_general(left, right, (((0,), (0,)), ((), ())), preferred_element_type=f32)
+
+
+def among(block, at, total_rows):
+    parts = []
+    if at > 0:
+        parts.append(jnp.zeros((at, block.shape[1]), block.dtype))
+    parts.append(block)
+    if at + block.shape[0] < total_rows:
+        parts.append(jnp.zeros((total_rows - at - block.shape[0], block.shape[1]), block.dtype))
+    return jnp.concatenate(parts, axis=0)
+
+
+def spaced(value, heads):
+    rows, columns = value.shape
+    each = columns // heads
+    lane = lax.broadcasted_iota(jnp.int32, (rows, columns), 1)
+    return jnp.concatenate(
+        [jnp.where((lane >= h * each) & (lane < (h + 1) * each), value, jnp.zeros_like(value)) for h in range(heads)],
+        axis=0)
 
 
 def round_up(value, step):
@@ -73,36 +96,30 @@
         "downg": vmem((H, F // H, D), bf16),
         "smallg": vmem((H, 4, 128), f32),
         "w2": vmem((H * C, D), bf16),
-        "w2t": vmem((D, H * C), bf16),
         "upcat": vmem((D, F), bf16),
         "projw": vmem((D, D), bf16),
         "bias": vmem((H, T, L), f32),
         "dbias": vmem((H, T, L), f32),
         "rowmask": vmem((T, D), f32),
-        "eye": vmem((D, D), bf16),
-        "eyet": vmem((T, L), bf16),
         "onehot": vmem((L, L), bf16),
         "xpad": vmem((n, L, D), bf16),
-        "mt": vmem((n, H * C, L), bf16),
+        "qt": vmem((n, H * KEY, L), bf16),
+        "knat": vmem((n, T, H * KEY), bf16),
         "vnat": vmem((n, T, H * VAL), bf16),
-        "qbd": vmem((H * KEY, H * L), bf16),
-        "dabd": vmem((H * VAL, H * L), bf16),
+        "tmp": vmem((z.group, T, D), f32),
         "p": vmem((n, H, T, L), bf16),
         "linv": vmem((n, H, 1, L), f32),
         "att": vmem((n, H * VAL, L), f32),
         "act": vmem((n, H * VAL, L), bf16),
         "proj": vmem((n, T, D), f32),
-        "res": vmem((n, T, D), bf16),
         "hid": vmem((n, T, F), f32),
         "slope": vmem((n, T, F), f32),
         "act2": vmem((n, T, F), bf16),
         "out": vmem((n, T, D), f32),
         "u": vmem((n, T, D), f32),
         "gproj": vmem((n, L, D), bf16),
-        "tmp": vmem((T, D), f32),
         "osend": vmem((H, n, z.share, D), bf16),
         "tsend": vmem((H, n, z.share, D), bf16),
-        "dmt": vmem((H * C, L), bf16),
         "gdown": vmem((D, F), f32),
         "gup": vmem((D, F), f32),
         "gpr": vmem((D, D), f32),
@@ -122,14 +139,13 @@
         "gl2r": vmem((B, z.rl // B, 128), f32),
         "gl3": vmem((B, z.rl // B, 128), f32),
         "loc": dma((8,)),
-        "hs": dma((9, H)),
-        "hr": dma((9, H)),
-        "ass": dma((6, z.ports)),
-        "asr": dma((6, z.ports)),
-        "cns": dma((B,)),
-        "cnr": dma((B,)),
-        "gbs": dma((4, B)),
-        "gbr": dma((4, B)),
+        "hs": dma((9,)),
+        "hr": dma((9,)),
+        "ass": dma((12,)),
+        "asr": dma((12,)),
+        "bs": dma((7,)),
+        "br": dma((7,)),
+        "ready": pltpu.SemaphoreType.REGULAR,
     }
 
 
@@ -149,13 +165,20 @@
 
     def to_head(src, dst, k, j):
         return pltpu.make_async_remote_copy(
-            src_ref=src, dst_ref=dst, send_sem=s.hs.at[k, j], recv_sem=s.hr.at[k, j],
-            device_id={"head": lax.rem(me_h + j, H)}, device_id_type=MESH)
-
-    def to_batch(src, dst, send, recv, j):
+            src_ref=src, dst_ref=dst, send_sem=s.hs.at[k], recv_sem=s.hr.at[k],
+            device_id={"head": head_peers[j]}, device_id_type=MESH)
+
+    def to_batch(src, dst, k, peer):
         return pltpu.make_async_remote_copy(
-            src_ref=src, dst_ref=dst, send_sem=send, recv_sem=recv,
-            device_id={"batch": lax.rem(me_b + j, B)}, device_id_type=MESH)
+            src_ref=src, dst_ref=dst, send_sem=s.bs.at[k], recv_sem=s.br.at[k],
+            device_id={"batch": peer}, device_id_type=MESH)
+
+    head_peers = [lax.rem(me_h + j, H) for j in range(H)]
+    core = lax.rem(me_b, 2)
+    sibling = me_b + 1 - 2 * core
+
+    def done(copies):
+        copies.wait()
 
     def around(size, step):
         if size <= 8:
@@ -181,59 +204,57 @@
         pairs = [(a, b) for a in range(H) for b in range(B) if a or b]
         return sorted(pairs, key=lambda p: -(p[0] % 2 + p[0] // 2 + (2 if p[1] > 1 else p[1] / 4)))
 
-    def at_offset(offset):
-        a, b = offset
+    def at_offset(a, b):
         x, y = lax.rem(me_h, 2), lax.div(me_h, 2)
         other = (y + a // 2 - 2 * y * (a // 2)) * 2 + x + a % 2 - 2 * x * (a % 2)
         return {"head": other, "batch": lax.rem(me_b + b, B)}
 
     barrier = pltpu.get_barrier_semaphore()
-    if z.direct:
-        for offset in everyone():
-            pl.semaphore_signal(barrier, inc=1, device_id=at_offset(offset), device_id_type=MESH)
-    else:
-        around(H, lambda j: pl.semaphore_signal(
-            barrier, inc=1, device_id={"head": lax.rem(me_h + j, H)}, device_id_type=MESH))
+    for j in range(1, H):
+        pl.semaphore_signal(barrier, inc=1, device_id={"head": head_peers[j]}, device_id_type=MESH)
+
+    def greet(semaphore):
         around(B, lambda j: pl.semaphore_signal(
-            barrier, inc=1, device_id={"batch": lax.rem(me_b + j, B)}, device_id_type=MESH))
+            semaphore, inc=1, device_id={"batch": lax.rem(me_b + j, B)}, device_id_type=MESH))
+
+    greet(barrier)
+    targets = [at_offset(*pair) for pair in everyone()] if z.direct else []
 
     s.smallg[me_h] = jnp.concatenate(
         [gain_2[...], shift_2[...], table[:, 0:128], jnp.concatenate(
             [table[:, 128:length], jnp.zeros((1, 256 - length), f32)], axis=1)], axis=0)
     c_qkv.wait()
     s.qkvg[me_h] = qkv_32[...].astype(bf16)
+    up_rows = pl.ds(pl.multiple_of(core * (D // 2), D // 2), D // 2)
+    down_rows = pl.ds(pl.multiple_of(core * (FH // 2), FH // 2), FH // 2)
     c_up.wait()
-    s.upcat[:, own] = up_32[...].astype(bf16)
+    s.upcat[up_rows, own] = s.gup[up_rows, 0:FH].astype(bf16)
     c_down.wait()
-    s.downg[me_h] = down_32[...].astype(bf16)
+    s.downg[me_h, down_rows] = s.gdown[down_rows, 0:D].astype(bf16)
 
     s.cnt[me_b] = jnp.full((1, 128), count[0]).astype(f32)
-    pl.semaphore_wait(barrier, H * B - 1 if z.direct else H - 1 + B - 1)
-
-    shared = (s.qkvg.at[me_h], s.smallg.at[me_h], s.upcat.at[:, own], s.downg.at[me_h])
-
-    def weight_copy(k, j):
-        return to_head(shared[k], shared[k], k, j)
-
-    for k in range(4):
+    pl.semaphore_wait(barrier, H - 1 + B - 1)
+
+    shared = (s.qkvg.at[me_h], s.smallg.at[me_h], s.upcat.at[up_rows, own], s.downg.at[me_h, down_rows])
+    for k in (1, 0, 2, 3):
         for j in range(1, H):
-            weight_copy(k, j).start()
-    def cot_copy(j):
-        peer = lax.rem(me_h + j, H)
-        return to_head(cot.at[:, pl.ds(window(peer), 16)], s.ct.at[pl.ds(me_h * share, share)], 4, j)
-
-    def count_copy(j):
-        return to_batch(s.cnt.at[me_b], s.cnt.at[me_b], s.cns.at[j], s.cnr.at[j], j)
-
-    around(B, lambda j: count_copy(j).start())
-    for j in range(1, H):
-        cot_copy(j).start()
+            to_head(shared[k], shared[k], k, j).start()
+    greet(s.ready)
+
+    cuts = (0, share // 2, share * 5 // 6, share)
+
+    def send_cotangent(piece):
+        low, high = cuts[piece], cuts[piece + 1]
+        for j in range(1, H):
+            to_head(cot.at[pl.ds(low, high - low), pl.ds(window(head_peers[j]), 16)],
+                    s.ct.at[pl.ds(me_h * share + low, high - low)], 4, j).start()
+
+    around(B, lambda j: to_batch(s.cnt.at[me_b], s.cnt.at[me_b], 0, lax.rem(me_b + j, B)).start())
+    send_cotangent(0)
     c_cot = local(cot.at[:, pl.ds(window(me_h), 16)], s.ct.at[pl.ds(me_h * share, share)], 5)
 
     row_at = lax.broadcasted_iota(jnp.int32, (L, L), 0)
     lane_at = lax.broadcasted_iota(jnp.int32, (L, L), 1)
-    s.eye[...] = jnp.where(row_at == lane_at, 1.0, 0.0).astype(bf16)
-    s.eyet[...] = jnp.where((row_at == lane_at) & (row_at < length), 1.0, 0.0)[0:T].astype(bf16)
     s.rowmask[...] = jnp.where(row_at < length, 1.0, 0.0)[0:T]
     place_lane = jnp.broadcast_to(
         jnp.concatenate([place[...].astype(f32), jnp.zeros((1, L - length), f32)], axis=1), (L, L))
@@ -250,9 +271,6 @@
     offsets = jnp.abs(rows_s - rows_t) * SIDE + jnp.abs(cols_s - cols_t)
     for h in range(H):
         s.dbias[h] = jnp.zeros((T, L), f32)
-    s.qbd[...] = jnp.zeros(s.qbd.shape, bf16)
-    s.dabd[...] = jnp.zeros(s.dabd.shape, bf16)
-    s.dmt[...] = jnp.zeros(s.dmt.shape, bf16)
     s.gdown[...] = jnp.zeros(s.gdown.shape, f32)
     s.gup[...] = jnp.zeros(s.gup.shape, f32)
     s.gqkv[...] = jnp.zeros(s.gqkv.shape, f32)
@@ -289,53 +307,60 @@
 
     lax.fori_loop(0, T // 16, enter_tokens, 0)
 
-    for k in range(2):
-        for j in range(1, H):
-            weight_copy(k, j).wait()
+    some = pl.ds(0, H - 1)
+    done(to_head(s.smallg.at[some], s.smallg.at[some], 1, 1))
+    for h in range(H):
+        line = jnp.concatenate([s.smallg[h, 2:3, :], s.smallg[h, 3:4, :]], axis=1)
+        s.bias[h] = jnp.where(row_at[0:T] < length, lookup(line, offsets) * LOG2E, -1e30)
+    done(to_head(s.qkvg.at[some], s.qkvg.at[some], 0, 1))
     for h in range(H):
         s.w2[h * KEY : (h + 1) * KEY] = s.qkvg[h, 0:KEY]
         s.w2[(H + h) * KEY : (H + h + 1) * KEY] = s.qkvg[h, KEY : 2 * KEY]
         at = 2 * H * KEY + h * VAL
         s.w2[at : at + VAL] = s.qkvg[h, 2 * KEY : C]
-        line = jnp.concatenate([s.smallg[h, 2:3, :], s.smallg[h, 3:4, :]], axis=1)
-        s.bias[h] = jnp.where(row_at[0:T] < length, lookup(line, offsets) * LOG2E, -1e30)
 
     scale = KEY**-0.5
     KH, VH = H * KEY, H * VAL
 
     def attend(i, carry):
         first, second = carry
-        x = s.xpad[i]
-        mixed = nt(s.w2[...], x).astype(bf16)
-        s.mt[i] = mixed
-        natural = nt(x[0:T], s.w2[KH : H * C]).astype(bf16)
-        s.vnat[i] = natural[:, KH:]
-        keys = natural[:, 0:KH]
+        at = [i * z.group + u for u in range(z.group)]
+        mixed, scores = [], []
+        for j in at:
+            x = s.xpad[j]
+            mixed.append(nt(s.w2[...], x).astype(bf16))
+            s.qt[j] = mixed[-1][0:KH]
+            natural = nt(x[0:T], s.w2[KH : H * C]).astype(bf16)
+            s.knat[j] = natural[:, 0:KH]
+            s.vnat[j] = natural[:, KH:]
+            scores.append(natural[:, 0:KH])
+        for u in range(z.group):
+            scores[u] = nn(spaced(scores[u], H), mixed[u][0:KH])
         for h in range(H):
-            s.qbd[h * KEY : (h + 1) * KEY, h * L : (h + 1) * L] = mixed[h * KEY : (h + 1) * KEY]
-        for h in range(H):
-            scores = nn(keys, s.qbd[:, h * L : (h + 1) * L]) * (scale * LOG2E) + s.bias[h]
-            raised = jnp.exp2(scores - jnp.max(scores, axis=0, keepdims=True))
-            inverse = 1.0 / total(raised)
-            s.linv[i, h] = inverse
-            low = raised.astype(bf16)
-            s.p[i, h] = low
-            values = mixed[2 * KH + h * VAL : 2 * KH + (h + 1) * VAL, 0:T]
-            attended = nn(values, low) * inverse
-            s.att[i, h * VAL : (h + 1) * VAL] = attended
-            s.act[i, h * VAL : (h + 1) * VAL] = (attended * sigmoid(attended)).astype(bf16)
-        active = nt(s.eyet[...], s.act[i]).astype(bf16)
-        projected = nn(active, s.projw[...])
-        s.proj[i] = projected
-        return first + fold(projected), second + fold(projected * projected)
+            for u, j in enumerate(at):
+                logits = scores[u][h * T : (h + 1) * T] * (scale * LOG2E) + s.bias[h]
+                raised = jnp.exp2(logits - jnp.max(logits, axis=0, keepdims=True))
+                inverse = 1.0 / total(raised)
+                s.linv[j, h] = inverse
+                low = raised.astype(bf16)
+                s.p[j, h] = low
+                values = mixed[u][2 * KH + h * VAL : 2 * KH + (h + 1) * VAL, 0:T]
+                attended = nn(values, low) * inverse
+                s.att[j, h * VAL : (h + 1) * VAL] = attended
+                s.act[j, h * VAL : (h + 1) * VAL] = (attended * sigmoid(attended)).astype(bf16)
+        for j in at:
+            projected = tn(s.act[j], s.projw[...])[0:T] * s.rowmask[...]
+            s.proj[j] = projected
+            first, second = first + fold(projected), second + fold(projected * projected)
+        return first, second
 
     def zeros(width):
         return jnp.zeros((8, width), f32)
 
-    def port(k, src, slot, offset, j):
+    def port(k, src, dst, device):
         return pltpu.make_async_remote_copy(
-            src_ref=src, dst_ref=slot, send_sem=s.ass.at[k, j], recv_sem=s.asr.at[k, j],
-            device_id=offset, device_id_type=MESH)
+            src_ref=src, dst_ref=dst, send_sem=s.ass.at[k], recv_sem=s.asr.at[k],
+            device_id=device, device_id_type=MESH)
 
     def sum_slots(buf, size):
         if size <= 32:
@@ -344,13 +369,6 @@
                 whole = whole + buf[b]
             return whole
         return lax.fori_loop(1, size, lambda b, c: c + buf[b], buf[0])
-
-    def sum_copies(k):
-        buf = z.bufs(s, k)[0]
-        if z.direct:
-            me = me_h * B + me_b
-            return [port(k, buf.at[me], buf.at[me], at_offset(o), j) for j, o in enumerate(everyone())]
-        return [port(k, buf.at[me_h], buf.at[me_h], {"head": lax.rem(me_h + j, H)}, j) for j in range(1, H)]
 
     def start_sum(k, rows):
         buf = z.bufs(s, k)[0]
@@ -360,21 +378,21 @@
             for c in range(row.shape[1] // 128):
                 buf[me, r : r + 1, :] = row[:, c * 128 : (c + 1) * 128]
                 r += 1
-        for copy in sum_copies(k):
-            copy.start()
+        for target in targets if z.direct else [{"head": p} for p in head_peers[1:]]:
+            port(k, buf.at[me], buf.at[me], target).start()
 
     def finish_sum(k, width):
-        for copy in sum_copies(k):
-            copy.wait()
+        others = z.bufs(s, k)[0].at[pl.ds(0, H * B - 1 if z.direct else H - 1)]
+        done(port(k, others, others, {"head": head_peers[1]}))
         bufs = z.bufs(s, k)
         if z.direct:
             whole = sum_slots(bufs[0], H * B)
         else:
             bufs[1][me_b] = sum_slots(bufs[0], H)
-            around(B, lambda j: port(
-                k, bufs[1].at[me_b], bufs[1].at[me_b], {"batch": lax.rem(me_b + j, B)}, H + j).start())
-            around(B, lambda j: port(
-                k, bufs[1].at[me_b], bufs[1].at[me_b], {"batch": lax.rem(me_b + j, B)}, H + j).wait())
+            mine = bufs[1].at[me_b]
+            around(B, lambda j: port(k + 6, mine, mine, {"batch": lax.rem(me_b + j, B)}).start())
+            others = bufs[1].at[pl.ds(0, B - 1)]
+            done(port(k + 6, others, others, {"batch": lax.rem(me_b + 1, B)}))
             whole = sum_slots(bufs[1], B)
         step = width // 128
         return [
@@ -382,20 +400,24 @@
             for r in range(0, whole.shape[0], step)
         ]
 
-    first, second = lax.fori_loop(0, n, attend, (zeros(D), zeros(D)))
+    first, second = lax.fori_loop(0, n // z.group, attend, (zeros(D), zeros(D)))
+    pl.semaphore_wait(s.ready, B - 1)
+    some_rows = pl.ds(0, D // 2)
+    done(to_head(s.upcat.at[some_rows, pl.ds(0, FH * (H - 1))], s.upcat.at[some_rows, pl.ds(0, FH * (H - 1))], 2, 1))
+    down_some = s.downg.at[some, pl.ds(0, FH // 2)]
+    done(to_head(down_some, down_some, 3, 1))
+    halves = (s.upcat.at[up_rows, :], s.downg.at[:, down_rows])
+    for k in range(2):
+        to_batch(halves[k], halves[k], k + 1, sibling).start()
     start_sum(0, [total(first), total(second)])
-    for j in range(1, H):
-        cot_copy(j).wait()
-    c_cot.wait()
-    lax.fori_loop(0, T // 16, enter_cotangent, 0)
-    for k in range(2, 4):
-        for j in range(1, H):
-            weight_copy(k, j).wait()
+    send_cotangent(1)
+    for k in range(2):
+        to_batch(halves[k], halves[k], k + 1, sibling).wait()
     down = s.downg[...].reshape(F, D)
-    s.w2t[...] = nt(s.eye[...], s.w2[...]).astype(bf16)
     gain_2w = jnp.concatenate([s.smallg[h, 0:1, :] for h in range(H)], axis=1)
     shift_2w = jnp.concatenate([s.smallg[h, 1:2, :] for h in range(H)], axis=1)
-    around(B, lambda j: count_copy(j).wait())
+    others = s.cnt.at[pl.ds(0, B - 1)]
+    done(to_batch(others, others, 0, sibling))
     seen_part = sum_slots(s.cnt, B) * float(length)
     seen_row = jnp.concatenate([seen_part] * (D // 128), axis=1)
     sums = finish_sum(0, D)
@@ -409,19 +431,35 @@
     a_1 = gain_1[...] * inverse_1
     b_1 = shift_1[...] - mean_1 * a_1
 
+    G = z.group
+    GT = G * T
+
+    def group(ref, i):
+        return ref[pl.ds(i * G, G), 0:T].reshape(GT, ref.shape[2])
+
+    def put(ref, i, value):
+        ref[pl.ds(i * G, G), 0:T] = value.reshape(G, T, value.shape[1])
+
+    def mask_of(i):
+        return jnp.concatenate([s.rowmask[...] * valid_of(i * G + u) for u in range(G)], axis=0)
+
     def residual_of(i):
-        return s.xpad[i, 0:T].astype(f32) + (s.proj[i] * a_1 + (b_1 * valid_of(i)) * s.rowmask[...])
+        return group(s.xpad, i).astype(f32) + (group(s.proj, i) * a_1 + b_1 * mask_of(i))
 
     def enter(i, carry):
         first, second = carry
         residual = residual_of(i).astype(bf16)
-        s.res[i] = residual
         hidden = nn(residual, s.upcat[...])
-        s.hid[i] = hidden
+        put(s.hid, i, hidden)
         return first + fold(hidden), second + fold(hidden * hidden)
 
-    first, second = lax.fori_loop(0, n, enter, (zeros(F), zeros(F)))
+    first, second = lax.fori_loop(0, n // G, enter, (zeros(F), zeros(F)))
     start_sum(1, [total(first), total(second)])
+    send_cotangent(2)
+    others = s.ct.at[pl.ds(0, share * (H - 1))]
+    done(to_head(others, others, 4, 1))
+    c_cot.wait()
+    lax.fori_loop(0, T // 16, enter_cotangent, 0)
     sums = finish_sum(1, F)
     mean_2, inverse_2 = moments(sums[0], sums[1], seen_wide)
     a_2 = gain_2w * inverse_2
@@ -429,21 +467,20 @@
 
     def leave(i, carry):
         one, two, three, four = carry
-        shaped = s.hid[i] * a_2 + b_2
+        shaped = group(s.hid, i) * a_2 + b_2
         gate = sigmoid(shaped)
         active = shaped * gate
-        s.slope[i] = gate + active * (1.0 - gate)
+        put(s.slope, i, gate + active * (1.0 - gate))
         low = active.astype(bf16)
-        s.act2[i] = low
+        put(s.act2, i, low)
         outgoing = nn(low, down)
-        s.out[i] = outgoing
-        valid = valid_of(i)
-        upstream = s.u[i]
-        masked = outgoing * (s.rowmask[...] * valid)
+        put(s.out, i, outgoing)
+        upstream = group(s.u, i)
+        masked = outgoing * mask_of(i)
         return (one + fold(masked), two + fold(masked * outgoing), three + fold(upstream),
                 four + fold(upstream * outgoing))
 
-    sums = lax.fori_loop(0, n, leave, (zeros(D), zeros(D), zeros(D), zeros(D)))
+    sums = lax.fori_loop(0, n // G, leave, (zeros(D), zeros(D), zeros(D), zeros(D)))
     start_sum(2, [total(v) for v in sums])
     sums = finish_sum(2, D)
     mean_3, inverse_3 = moments(sums[0], sums[1], seen_row)
@@ -461,24 +498,33 @@
 
     def back_leave(i, carry):
         one, two = carry
-        mask = s.rowmask[...] * valid_of(i)
-        grad = (s.u[i] * s_3 + (s.out[i] * v_3 + r_3) * mask).astype(bf16)
-        s.gproj[i, 0:T, :] = grad
-        shaped = nt(grad, down) * s.slope[i]
-        s.slope[i] = shaped
-        return one + fold(shaped), two + fold(shaped * s.hid[i])
+        grad = (group(s.u, i) * s_3 + (group(s.out, i) * v_3 + r_3) * mask_of(i)).astype(bf16)
+        put(s.gproj, i, grad)
+        shaped = nt(grad, down) * group(s.slope, i)
+        put(s.slope, i, shaped)
+        return one + fold(shaped), two + fold(shaped * group(s.hid, i))
 
     def down_gradient(i, carry):
-        turned = nt(s.eye[...], s.gproj[i, 0:T, :]).astype(bf16)
-        s.gdown[...] += nn(turned, s.act2[i])
-        s.tmp[...] = (residual_of(i) + (s.out[i] * a_3 + b_3)) * valid_of(i)
-        for q in range(H):
-            s.osend[q, i] = s.tmp[q * share : (q + 1) * share, :].astype(bf16)
+        s.gdown[...] += tn(group(s.gproj, i), group(s.act2, i))
         return carry
 
-    first, second = lax.fori_loop(0, n, back_leave, (zeros(F), zeros(F)))
+    def output(i, carry):
+        s.tmp[...] = ((residual_of(i) + (group(s.out, i) * a_3 + b_3)) * mask_of(i)).reshape(G, T, D)
+        for u in range(G):
+            for q in range(H):
+                s.osend[q, i * G + u] = s.tmp[u, q * share : (q + 1) * share, :].astype(bf16)
+        return carry
+
+    def send_output(i):
+        to = out_o.at[pl.ds(me_h * n + i * G, G)]
+        for j in range(1, H):
+            to_head(s.osend.at[head_peers[j], pl.ds(i * G, G)], to, 5, j).start()
+
+    first, second = lax.fori_loop(0, n // G, back_leave, (zeros(F), zeros(F)))
     start_sum(3, [total(first), total(second)])
-    lax.fori_loop(0, n, down_gradient, 0)
+    lax.fori_loop(0, n // G, output, 0)
+    send_output(0)
+    lax.fori_loop(0, n // G, down_gradient, 0)
     sums = finish_sum(3, F)
 
     sum_shift_2 = sums[0]
@@ -489,51 +535,59 @@
 
     def back_enter(i, carry):
         one, two = carry
-        mask = s.rowmask[...] * valid_of(i)
-        grad = (s.slope[i] * s_2 + s.hid[i] * v_2 + r_2 * jnp.concatenate([mask] * (F // D), axis=1)).astype(bf16)
-        s.act2[i] = grad
-        upstream = s.u[i] + nt(grad, s.upcat[...])
-        s.u[i] = upstream
-        return one + fold(upstream), two + fold(upstream * s.proj[i])
-
-    first, second = lax.fori_loop(0, n, back_enter, (zeros(D), zeros(D)))
+        mask = jnp.concatenate([mask_of(i)] * (F // D), axis=1)
+        grad = (group(s.slope, i) * s_2 + group(s.hid, i) * v_2 + r_2 * mask).astype(bf16)
+        put(s.act2, i, grad)
+        upstream = group(s.u, i) + nt(grad, s.upcat[...])
+        put(s.u, i, upstream)
+        return one + fold(upstream), two + fold(upstream * group(s.proj, i))
+
+    first, second = lax.fori_loop(0, n // G, back_enter, (zeros(D), zeros(D)))
     start_sum(4, [total(first), total(second)])
 
     def up_gradient(i, carry):
-        turned = nt(s.eye[...], s.res[i]).astype(bf16)
-        s.gup[...] += nn(turned, s.act2[i])
+        s.gup[...] += tn(residual_of(i).astype(bf16), group(s.act2, i))
         return carry
 
-    lax.fori_loop(0, n, up_gradient, 0)
+    if n // G > 1:
+        send_output(1)
+    lax.fori_loop(0, n // G, up_gradient, 0)
     sums = finish_sum(4, D)
-    for j in range(1, H):
-        to_head(s.osend.at[lax.rem(me_h + j, H)], out_o.at[pl.ds(me_h * n, n)], 5, j).start()
     c_out = local(s.osend.at[me_h], out_o.at[pl.ds(me_h * n, n)], 6)
     sum_shift_1 = sums[0]
     sum_gain_1 = inverse_1 * (sums[1] - mean_1 * sum_shift_1)
     s_1, v_1, r_1 = back(gain_1[...], mean_1, inverse_1, sum_shift_1, sum_gain_1, seen_row)
 
     def back_project(i, carry):
-        mask = s.rowmask[...] * valid_of(i)
-        grad = (s.u[i] * s_1 + s.proj[i] * v_1 + r_1 * mask).astype(bf16)
-        s.gproj[i, 0:T, :] = grad
-        s.gpr[...] += nn(s.act[i], s.gproj[i])
+        grad = (group(s.u, i) * s_1 + group(s.proj, i) * v_1 + r_1 * mask_of(i)).astype(bf16)
+        put(s.gproj, i, grad)
+        whole = s.gpr[...]
+        for u in range(G):
+            whole = whole + nn(s.act[i * G + u], s.gproj[i * G + u])
+        s.gpr[...] = whole
         return carry
 
-    lax.fori_loop(0, n, back_project, 0)
+    lax.fori_loop(0, n // G, back_project, 0)
 
     def shares(buffer, k):
         for j in range(1, H):
-            yield to_head(buffer[0].at[lax.rem(me_h + j, H)], buffer[1].at[me_h], k, j)
+            to_head(buffer[0].at[head_peers[j]], buffer[1].at[me_h], k, j).start()
+
+    def shares_done(buffer, k):
+        done(to_head(buffer[0].at[some], buffer[1].at[some], k, 1))
 
     def head_sum(buffer):
         whole = buffer[0][me_h].astype(f32)
         for j in range(1, H):
-            whole = whole + buffer[1][lax.rem(me_h + j, H)].astype(f32)
+            whole = whole + buffer[1][head_peers[j]].astype(f32)
         return whole
 
-    def spread(src, dst, k, act):
-        around(B, lambda j: act(to_batch(src(lax.rem(me_b + j, B)), dst, s.gbs.at[k, j], s.gbr.at[k, j], j)))
+    def spread(src, dst, k):
+        around(B, lambda j: to_batch(src(lax.rem(me_b + j, B)), dst, k, lax.rem(me_b + j, B)).start())
+
+    def spread_done(src, dst, k):
+        others = pl.ds(0, B - 1)
+        done(to_batch(src.at[others], dst.at[others], k, sibling))
 
     def batch_sum(own, received):
         if B <= 8:
@@ -551,52 +605,72 @@
             s.ge1[h, at : at + PH, :] = s.gpr[h * PH : (h + 1) * PH, half * 128 : (half + 1) * 128].astype(bf16)
         if z.re > 2 * D + PH * (D // 128):
             s.ge1[h, 2 * D + PH * (D // 128) :, :] = jnp.zeros((z.re - 2 * D - PH * (D // 128), 128), bf16)
-    for copy in shares((s.ge1, s.ge1r), 7):
-        copy.start()
-
-    def back_attend(i, carry):
-        slope_gate = sigmoid(s.att[i])
-        att = s.att[i]
-        active = att * slope_gate
-        gact = nt(s.projw[...], s.gproj[i]) * (slope_gate + active * (1.0 - slope_gate))
+    shares((s.ge1, s.ge1r), 7)
+    for i in range(2, n // G):
+        send_output(i)
+
+    GB = z.group_back
+
+    def back_attend(i, carry, send=True):
+        at = [i * GB + u for u in range(GB)]
+        lows, deltas, products = [], [], []
+        for j in at:
+            att = s.att[j]
+            gate = sigmoid(att)
+            active = att * gate
+            gact = nt(s.projw[...], s.gproj[j]) * (gate + active * (1.0 - gate))
+            low, delta = [], []
+            for h in range(H):
+                rows = slice(h * VAL, (h + 1) * VAL)
+                grad = gact[rows] * s.linv[j, h]
+                low.append(grad.astype(bf16))
+                delta.append(total(grad * att[rows]))
+            lows.append(low)
+            deltas.append(delta)
+            products.append(nn(spaced(s.vnat[j], H), jnp.concatenate(low, axis=0)))
+        grads = [[] for _ in at]
         for h in range(H):
-            rows = slice(h * VAL, (h + 1) * VAL)
-            grad = gact[rows] * s.linv[i, h]
-            low = grad.astype(bf16)
-            s.dabd[rows, h * L : (h + 1) * L] = low
-            delta = total(grad * att[rows])
-            weights_low = s.p[i, h]
-            gscores = weights_low.astype(f32) * (nn(s.vnat[i], s.dabd[:, h * L : (h + 1) * L]) - delta)
-            s.dbias[h] += gscores
-            glow = gscores.astype(bf16)
-            q_rows = slice(h * KEY, (h + 1) * KEY)
-            k_rows = slice(KH + h * KEY, KH + (h + 1) * KEY)
-            v_rows = slice(2 * KH + h * VAL, 2 * KH + (h + 1) * VAL)
-            s.dmt[q_rows, :] = (nn(s.mt[i, k_rows, 0:T], glow) * scale).astype(bf16)
-            s.dmt[k_rows, 0:T] = (nt(s.mt[i, q_rows, :], glow) * scale).astype(bf16)
-            s.dmt[v_rows, 0:T] = nt(low, weights_low).astype(bf16)
-        s.gqkv[...] += nn(s.dmt[...], s.xpad[i])
-        turned = nn(s.w2t[...], s.dmt[...]).astype(bf16)
-        s.tmp[...] = s.u[i] + nt(s.eyet[...], turned)
-        for q in range(H):
-            s.tsend[q, i] = s.tmp[q * share : (q + 1) * share, :].astype(bf16)
+            whole = None
+            for u, j in enumerate(at):
+                gscores = s.p[j, h].astype(f32) * (products[u][h * T : (h + 1) * T] - deltas[u][h])
+                whole = gscores if whole is None else whole + gscores
+                grads[u].append(gscores.astype(bf16))
+            s.dbias[h] += whole
+        mixes = []
+        for u, j in enumerate(at):
+            queries = s.qt[j]
+            near = jnp.concatenate(
+                [among(queries[h * KEY : (h + 1) * KEY], h * KEY, KH) for h in range(H)], axis=1)
+            far = jnp.concatenate([among(lows[u][h], h * VAL, VH) for h in range(H)], axis=1)
+            grad_k = nt(jnp.concatenate(grads[u], axis=1), near) * scale
+            grad_v = nt(jnp.concatenate([s.p[j, h] for h in range(H)], axis=1), far)
+            grad_q = tn(jnp.concatenate(grads[u], axis=0), spaced(s.knat[j], H))[0:T] * scale
+            mixes.append(jnp.concatenate([v.astype(bf16) for v in (grad_q, grad_k, grad_v)], axis=1))
+        whole = s.gqkv[...]
+        for u, j in enumerate(at):
+            whole = whole + tn(mixes[u], s.xpad[j, 0:T])
+        s.gqkv[...] = whole
+        terms = nn(jnp.concatenate(mixes, axis=0), s.w2[...])
+        for u, j in enumerate(at):
+            s.tmp[u] = s.u[j] + terms[u * T : (u + 1) * T]
+            for q in range(H):
+                s.tsend[q, j] = s.tmp[u, q * share : (q + 1) * share, :].astype(bf16)
+        if send:
+            send_tokens(i)
+        return carry
+
+    def send_tokens(i):
+        to = tg_o.at[pl.ds(me_h * n + i * GB, GB)]
         for j in range(1, H):
-            to_head(s.tsend.at[lax.rem(me_h + j, H), i], tg_o.at[me_h * n + i], 6, j).start()
-        pltpu.make_async_copy(s.tsend.at[me_h, i], tg_o.at[me_h * n + i], s.loc.at[7]).start()
-        return carry
-
-    lax.fori_loop(0, n // 2, back_attend, 0)
-
-    for copy in shares((s.ge1, s.ge1r), 7):
-        copy.wait()
+            to_head(s.tsend.at[head_peers[j], pl.ds(i * GB, GB)], to, 6, j).start()
+        pltpu.make_async_copy(s.tsend.at[me_h, pl.ds(i * GB, GB)], to, s.loc.at[7]).start()
+
+    last = n // GB - 1
+    lax.fori_loop(0, last, back_attend, 0)
+    shares_done((s.ge1, s.ge1r), 7)
     s.ge2[...] = head_sum((s.ge1, s.ge1r)).reshape(B, z.re // B, 128)
-    spread(lambda peer: s.ge2.at[peer], s.ge2r.at[me_b], 0, lambda c: c.start())
-
-    lax.fori_loop(n // 2, n, back_attend, 0)
-
-    spread(lambda peer: s.ge2.at[peer], s.ge2r.at[me_b], 0, lambda c: c.wait())
-    s.ge3[me_b] = batch_sum(s.ge2[me_b], s.ge2r)
-    spread(lambda peer: s.ge3.at[me_b], s.ge3.at[me_b], 1, lambda c: c.start())
+    spread(lambda peer: s.ge2.at[peer], s.ge2r.at[me_b], 3)
+    lax.fori_loop(last, last + 1, functools.partial(back_attend, send=False), 0)
 
     for h in range(H):
         for half in range(D // 128):
@@ -607,8 +681,11 @@
             s.gl1[h, at + 2 * KEY : at + C, :] = s.gqkv[2 * KH + h * VAL : 2 * KH + (h + 1) * VAL, lanes].astype(bf16)
         if z.rl > C * (D // 128):
             s.gl1[h, C * (D // 128) :, :] = jnp.zeros((z.rl - C * (D // 128), 128), bf16)
-    for copy in shares((s.gl1, s.gl1r), 8):
-        copy.start()
+    shares((s.gl1, s.gl1r), 8)
+    spread_done(s.ge2, s.ge2r, 3)
+    s.ge3[me_b] = batch_sum(s.ge2[me_b], s.ge2r)
+    spread(lambda peer: s.ge3.at[me_b], s.ge3.at[me_b], 4)
+    send_tokens(last)
 
     slot = lax.broadcasted_iota(jnp.int32, (T, L), 1)
     d_row, d_col = grid_of(slot)
@@ -635,15 +712,14 @@
         bias_rows.append(total(line * s.rowmask[...]))
     start_sum(5, bias_rows)
 
-    for copy in shares((s.gl1, s.gl1r), 8):
-        copy.wait()
+    shares_done((s.gl1, s.gl1r), 8)
     s.gl2[...] = head_sum((s.gl1, s.gl1r)).reshape(B, z.rl // B, 128)
-    spread(lambda peer: s.gl2.at[peer], s.gl2r.at[me_b], 2, lambda c: c.start())
+    spread(lambda peer: s.gl2.at[peer], s.gl2r.at[me_b], 5)
     for h, row in enumerate(finish_sum(5, L)):
         s.brow[h] = row
-    spread(lambda peer: s.gl2.at[peer], s.gl2r.at[me_b], 2, lambda c: c.wait())
+    spread_done(s.gl2, s.gl2r, 5)
     s.gl3[me_b] = batch_sum(s.gl2[me_b], s.gl2r)
-    spread(lambda peer: s.gl3.at[me_b], s.gl3.at[me_b], 3, lambda c: c.start())
+    spread(lambda peer: s.gl3.at[me_b], s.gl3.at[me_b], 6)
 
     small_o[...] = jnp.zeros(small_o.shape, f32)
     small_o[0:1, :] = sum_gain_1
@@ -654,14 +730,13 @@
     small_o[5:6, 0:FH] = s.srow[1:2, own]
     small_o[6:7, :] = s.brow[me_h]
 
-    spread(lambda peer: s.ge3.at[me_b], s.ge3.at[me_b], 1, lambda c: c.wait())
+    spread_done(s.ge3, s.ge3, 4)
     early_o[...] = s.ge3[...].reshape(z.re, 128)
-    spread(lambda peer: s.gl3.at[me_b], s.gl3.at[me_b], 3, lambda c: c.wait())
+    spread_done(s.gl3, s.gl3, 6)
     late_o[...] = s.gl3[...].reshape(z.rl, 128)
 
-    for j in range(1, H):
-        to_head(s.osend.at[lax.rem(me_h + j, H)], out_o.at[pl.ds(me_h * n, n)], 5, j).wait()
-        to_head(s.tsend.at[lax.rem(me_h + j, H)], tg_o.at[pl.ds(me_h * n, n)], 6, j).wait()
+    done(to_head(s.osend.at[some], out_o.at[pl.ds(0, n * (H - 1))], 5, 1))
+    done(to_head(s.tsend.at[some], tg_o.at[pl.ds(0, n * (H - 1))], 6, 1))
     c_out.wait()
     pltpu.make_async_copy(s.tsend.at[me_h], tg_o.at[pl.ds(me_h * n, n)], s.loc.at[7]).wait()
 
@@ -704,8 +779,9 @@
         H=H, B=B, C=qkv_weight.shape[1], share=cotangent.shape[1], length=length)
     z.re = round_up(2 * z.D + z.D // H * (z.D // 128), 8 * max(B, 2))
     z.rl = round_up(z.C * (z.D // 128), 8 * max(B, 2))
+    z.group = max(g for g in (1, 2, 3, 4) if z.n % g == 0)
+    z.group_back = max(g for g in (1, 2, 3) if z.n % g == 0)
     z.direct = H == 4 and B <= 8
-    z.ports = H * B if z.direct else H + B
     z.sums = {}
     for k, r in enumerate((2 * z.D, 2 * z.F, 4 * z.D, 2 * z.F, 2 * z.D, H * z.L)):
         z.sums["sum%d" % k] = pltpu.VMEM((H * B if z.direct else H, r // 128, 128), f32)

time: 140 us -> 106 us (0.76)
  Pallas kernels: 138 us -> 104 us
    pallas_call x1, Pallas kernels: 131 us -> 97.7 us  [on_device(): pl.pallas_call(functools.partial(block_kernel, z, tuple(scratch)), out_sh...]
where the time goes in v3:
time: 106 us
  Pallas kernels  104 us (98%)
  between operations  1.46 us (1%)
    pallas_call x1, Pallas kernels, on_device(): pl.pallas_call(functools.partial(block_kernel, z, tuple(scratch)), out_sh...  97.7 us
    pallas_call x1, Pallas kernels, on_device(): pl.pallas_call(functools.partial(finish_kernel, z), grid=(steps,), out_sh...  6.83 us

profile of v3, /device:TPU:0, one launch (start us, length us, event | category | flops | bytes accessed | tf_op | source)
XLA Modules:
  0.0 106.0 jit_solution(12791306634065209323)
XLA Ops:
  1.3 97.7 %shard_map.246 = (bf16[48,49,256]{2,1,0:T(8,128)(2,1)}, bf16[48,49,256]{2,1,0:T(8,128)(2,1)}, f32[640,128]{1,0:T(8,128)}, f32[256,128]{1,0:T(8,128)}, f32[8,256]{1,0:T(8,128)}) custom-call(bf16[196,48,256]{2,1,0:T(8,128)(2,1)} %bitcast.17, s32[1]{0:T(128)S(6)} %copy.28.refs_1_, s32[1,196]{1,0:T(1,128)} %bitcast.19, f32[1,128,256]{2,1,0:T(8,128)} %refs_3_.1, ...), custom_call_target="tpu_custom_call" | custom-call | tf_op jit(solution)/shard_map/pallas_call | solution.py:800
  99.0 6.8 %shard_map.247 = (f32[49,48,256]{2,1,0:T(8,128)}, f32[49,48,256]{2,1,0:T(8,128)}, f32[1,128,256]{2,1,0:T(8,128)}, f32[1,196]{1,0:T(1,128)}, f32[64,256]{1,0:T(8,...) custom-call(bf16[48,49,256]{2,1,0:T(8,128)(2,1)} %get-tuple-element., ...), custom_call_target="tpu_custom_call" | custom-call | tf_op jit(solution)/shard_map/pallas_call | solution.py:834

commit v4 on v3

--- a/solution.py
+++ b/solution.py
@@ -91,7 +91,10 @@
     return {
         "xt": vmem((T, 16, D), bf16),
         "ct": vmem((T, 16, D), bf16),
+        "cin": vmem((round_up(z.share, 4), H * n, D), bf16),
         "mix": vmem((n * 16, 256), bf16),
+        "unmix": vmem((n * 16, n * 16), bf16),
+        "deal": vmem((H * n * 4, H * n * 4), bf16),
         "qkvg": vmem((H, C, D), bf16),
         "downg": vmem((H, F // H, D), bf16),
         "smallg": vmem((H, 4, 128), f32),
@@ -199,6 +202,7 @@
 
     c_tok = local(tokens.at[:, pl.ds(window(me_h), 16)], s.xt.at[pl.ds(0, length)], 3)
     c_proj = local(proj_w, s.gpr, 4)
+    c_cot = local(cot, s.cin.at[pl.ds(0, share)], 6)
 
     def everyone():
         pairs = [(a, b) for a in range(H) for b in range(B) if a or b]
@@ -231,27 +235,6 @@
     s.upcat[up_rows, own] = s.gup[up_rows, 0:FH].astype(bf16)
     c_down.wait()
     s.downg[me_h, down_rows] = s.gdown[down_rows, 0:D].astype(bf16)
-
-    s.cnt[me_b] = jnp.full((1, 128), count[0]).astype(f32)
-    pl.semaphore_wait(barrier, H - 1 + B - 1)
-
-    shared = (s.qkvg.at[me_h], s.smallg.at[me_h], s.upcat.at[up_rows, own], s.downg.at[me_h, down_rows])
-    for k in (1, 0, 2, 3):
-        for j in range(1, H):
-            to_head(shared[k], shared[k], k, j).start()
-    greet(s.ready)
-
-    cuts = (0, share // 2, share * 5 // 6, share)
-
-    def send_cotangent(piece):
-        low, high = cuts[piece], cuts[piece + 1]
-        for j in range(1, H):
-            to_head(cot.at[pl.ds(low, high - low), pl.ds(window(head_peers[j]), 16)],
-                    s.ct.at[pl.ds(me_h * share + low, high - low)], 4, j).start()
-
-    around(B, lambda j: to_batch(s.cnt.at[me_b], s.cnt.at[me_b], 0, lax.rem(me_b + j, B)).start())
-    send_cotangent(0)
-    c_cot = local(cot.at[:, pl.ds(window(me_h), 16)], s.ct.at[pl.ds(me_h * share, share)], 5)
 
     row_at = lax.broadcasted_iota(jnp.int32, (L, L), 0)
     lane_at = lax.broadcasted_iota(jnp.int32, (L, L), 1)
@@ -290,7 +273,7 @@
         & (image_at + me_h * n < count[0]),
         1.0, 0.0).astype(bf16)
     s.xt[length:T] = jnp.zeros((T - length, 16, D), bf16)
-    s.ct[length:T] = jnp.zeros((T - length, 16, D), bf16)
+    s.u[:, T - 16 : T, :] = jnp.zeros((n, 16, D), f32)
     s.xpad[:, T:L, :] = jnp.zeros((n, L - T, D), bf16)
     s.gproj[:, T:L, :] = jnp.zeros((n, L - T, D), bf16)
     c_tok.wait()
@@ -300,12 +283,74 @@
         s.xpad[:, at, :] = nn(s.mix[...], s.xt[at].reshape(256, D)).astype(bf16).reshape(n, 16, D)
         return carry
 
-    def enter_cotangent(k, carry):
-        at = pl.ds(pl.multiple_of(k * 16, 16), 16)
-        s.u[:, at, :] = nn(s.mix[...], s.ct[at].reshape(256, D)).reshape(n, 16, D)
-        return carry
-
     lax.fori_loop(0, T // 16, enter_tokens, 0)
+
+
+    blocks = -(-share * n // 16)
+    step = n * 4 // 16
+
+    def over(value, divisor):
+        return lax.shift_right_logical(value * (65536 // divisor + 1), 16)
+
+    def square(size):
+        return (lax.broadcasted_iota(jnp.int32, (size, size), 0),
+                lax.broadcasted_iota(jnp.int32, (size, size), 1))
+
+    to, at = square(n * 16)
+    image_to = lax.shift_right_logical(to, 4)
+    s.unmix[...] = jnp.where(
+        (at == lax.bitwise_and(to, 15) * n + image_to) & (image_to + me_h * n < count[0]), 1.0, 0.0).astype(bf16)
+    to, at = square(H * n * 4)
+    owner = over(to, n * 4)
+    inside = to - owner * (n * 4)
+    token_to = over(inside, n)
+    s.deal[...] = jnp.where(
+        at == token_to * (H * n) + owner * n + inside - token_to * n, 1.0, 0.0).astype(bf16)
+    s.cin[share:] = jnp.zeros((s.cin.shape[0] - share, H * n, D), bf16)
+    c_cot.wait()
+
+    def deal(k, wide):
+        dealt = nn(s.deal[...], s.cin[pl.ds(k * 4, 4)].reshape(H * n * 4, D)).astype(bf16)
+        for h in range(H):
+            piece = dealt[h * n * 4 : h * n * 4 + wide * 16].reshape(wide, 16, D)
+            s.xt[pl.ds(h * blocks + k * step, wide)] = piece
+
+    lax.fori_loop(0, share // 4, lambda k, c: (deal(k, step), c)[1], 0)
+    if share % 4:
+        deal(share // 4, blocks - share // 4 * step)
+    own_blocks = pl.ds(me_h * blocks, blocks)
+    c_own = local(s.xt.at[own_blocks], s.ct.at[own_blocks], 5)
+
+    def enter_cotangent(q):
+        first = q * blocks
+        for k in range(share // 16):
+            rows = s.ct[first + k * n : first + (k + 1) * n].reshape(n * 16, D)
+            at = q * share + k * 16
+            s.u[:, at : at + 16, :] = nn(s.unmix[...], rows).reshape(n, 16, D)
+        rest = s.ct[first + share // 16 * n].astype(f32)
+        for i in range(n):
+            at = q * share + share // 16 * 16
+            s.u[i, at : at + 1, :] = rest[i : i + 1] * valid_of(i)
+
+    s.cnt[me_b] = jnp.full((1, 128), count[0]).astype(f32)
+    pl.semaphore_wait(barrier, H - 1 + B - 1)
+
+    shared = (s.qkvg.at[me_h], s.smallg.at[me_h], s.upcat.at[up_rows, own], s.downg.at[me_h, down_rows])
+    for k in (1, 0, 2, 3):
+        for j in range(1, H):
+            to_head(shared[k], shared[k], k, j).start()
+    greet(s.ready)
+
+    cuts = (0, blocks * 6 // 10, blocks)
+
+    def send_cotangent(piece):
+        low, high = cuts[piece], cuts[piece + 1]
+        for j in range(1, H):
+            to_head(s.xt.at[pl.ds(head_peers[j] * blocks + low, high - low)],
+                    s.ct.at[pl.ds(me_h * blocks + low, high - low)], 4, j).start()
+
+    around(B, lambda j: to_batch(s.cnt.at[me_b], s.cnt.at[me_b], 0, lax.rem(me_b + j, B)).start())
+    send_cotangent(0)
 
     some = pl.ds(0, H - 1)
     done(to_head(s.smallg.at[some], s.smallg.at[some], 1, 1))
@@ -455,11 +500,11 @@
 
     first, second = lax.fori_loop(0, n // G, enter, (zeros(F), zeros(F)))
     start_sum(1, [total(first), total(second)])
-    send_cotangent(2)
-    others = s.ct.at[pl.ds(0, share * (H - 1))]
+    others = s.ct.at[pl.ds(0, blocks * (H - 1))]
     done(to_head(others, others, 4, 1))
-    c_cot.wait()
-    lax.fori_loop(0, T // 16, enter_cotangent, 0)
+    c_own.wait()
+    for q in range(H):
+        enter_cotangent(q)
     sums = finish_sum(1, F)
     mean_2, inverse_2 = moments(sums[0], sums[1], seen_wide)
     a_2 = gain_2w * inverse_2
@@ -508,12 +553,20 @@
         s.gdown[...] += tn(group(s.gproj, i), group(s.act2, i))
         return carry
 
-    def output(i, carry):
+    def output(i):
         s.tmp[...] = ((residual_of(i) + (group(s.out, i) * a_3 + b_3)) * mask_of(i)).reshape(G, T, D)
         for u in range(G):
             for q in range(H):
                 s.osend[q, i * G + u] = s.tmp[u, q * share : (q + 1) * share, :].astype(bf16)
-        return carry
+
+    def early(at, parts):
+        for h, part in enumerate(parts):
+            s.ge1[h, at : at + part.shape[0], :] = part.astype(bf16)
+
+    def send_early(low, high):
+        rows = pl.ds(low, high - low)
+        for j in range(1, H):
+            to_head(s.ge1.at[head_peers[j], rows], s.ge1r.at[me_h, rows], 7, j).start()
 
     def send_output(i):
         to = out_o.at[pl.ds(me_h * n + i * G, G)]
@@ -522,9 +575,10 @@
 
     first, second = lax.fori_loop(0, n // G, back_leave, (zeros(F), zeros(F)))
     start_sum(3, [total(first), total(second)])
-    lax.fori_loop(0, n // G, output, 0)
+    output(0)
     send_output(0)
     lax.fori_loop(0, n // G, down_gradient, 0)
+    early(0, [s.gdown[:, h * FH : (h + 1) * FH] for h in range(H)])
     sums = finish_sum(3, F)
 
     sum_shift_2 = sums[0]
@@ -544,14 +598,17 @@
 
     first, second = lax.fori_loop(0, n // G, back_enter, (zeros(D), zeros(D)))
     start_sum(4, [total(first), total(second)])
+    send_early(0, D)
 
     def up_gradient(i, carry):
         s.gup[...] += tn(residual_of(i).astype(bf16), group(s.act2, i))
         return carry
 
-    if n // G > 1:
-        send_output(1)
     lax.fori_loop(0, n // G, up_gradient, 0)
+    early(D, [s.gup[:, h * FH : (h + 1) * FH] for h in range(H)])
+    send_early(D, 2 * D)
+    for i in range(1, n // G):
+        output(i)
     sums = finish_sum(4, D)
     c_out = local(s.osend.at[me_h], out_o.at[pl.ds(me_h * n, n)], 6)
     sum_shift_1 = sums[0]
@@ -597,21 +654,19 @@
             return whole
         return lax.fori_loop(1, B, lambda j, c: c + received[lax.rem(me_b + j, B)], own)
 
-    for h in range(H):
-        s.ge1[h, 0:D, :] = s.gup[:, h * FH : (h + 1) * FH].astype(bf16)
-        s.ge1[h, D : 2 * D, :] = s.gdown[:, h * FH : (h + 1) * FH].astype(bf16)
-        for half in range(D // 128):
-            at = 2 * D + half * PH
-            s.ge1[h, at : at + PH, :] = s.gpr[h * PH : (h + 1) * PH, half * 128 : (half + 1) * 128].astype(bf16)
-        if z.re > 2 * D + PH * (D // 128):
-            s.ge1[h, 2 * D + PH * (D // 128) :, :] = jnp.zeros((z.re - 2 * D - PH * (D // 128), 128), bf16)
-    shares((s.ge1, s.ge1r), 7)
-    for i in range(2, n // G):
+    for half in range(D // 128):
+        lanes = slice(half * 128, (half + 1) * 128)
+        early(2 * D + half * PH, [s.gpr[h * PH : (h + 1) * PH, lanes] for h in range(H)])
+    filled = 2 * D + D // 128 * PH
+    if z.re > filled:
+        s.ge1[:, filled:, :] = jnp.zeros((H, z.re - filled, 128), bf16)
+    send_early(2 * D, z.re)
+    for i in range(1, n // G):
         send_output(i)
 
     GB = z.group_back
 
-    def back_attend(i, carry, send=True):
+    def back_attend(i, carry):
         at = [i * GB + u for u in range(GB)]
         lows, deltas, products = [], [], []
         for j in at:
@@ -655,8 +710,14 @@
             s.tmp[u] = s.u[j] + terms[u * T : (u + 1) * T]
             for q in range(H):
                 s.tsend[q, j] = s.tmp[u, q * share : (q + 1) * share, :].astype(bf16)
-        if send:
-            send_tokens(i)
+        pl.when(i == 0)(lambda: send_tokens(0))
+
+        @pl.when(i == 1)
+        def _():
+            shares_done((s.ge1, s.ge1r), 7)
+            s.ge2[...] = head_sum((s.ge1, s.ge1r)).reshape(B, z.re // B, 128)
+            spread(lambda peer: s.ge2.at[peer], s.ge2r.at[me_b], 3)
+
         return carry
 
     def send_tokens(i):
@@ -665,12 +726,7 @@
             to_head(s.tsend.at[head_peers[j], pl.ds(i * GB, GB)], to, 6, j).start()
         pltpu.make_async_copy(s.tsend.at[me_h, pl.ds(i * GB, GB)], to, s.loc.at[7]).start()
 
-    last = n // GB - 1
-    lax.fori_loop(0, last, back_attend, 0)
-    shares_done((s.ge1, s.ge1r), 7)
-    s.ge2[...] = head_sum((s.ge1, s.ge1r)).reshape(B, z.re // B, 128)
-    spread(lambda peer: s.ge2.at[peer], s.ge2r.at[me_b], 3)
-    lax.fori_loop(last, last + 1, functools.partial(back_attend, send=False), 0)
+    lax.fori_loop(0, n // GB, back_attend, 0)
 
     for h in range(H):
         for half in range(D // 128):
@@ -685,7 +741,6 @@
     spread_done(s.ge2, s.ge2r, 3)
     s.ge3[me_b] = batch_sum(s.ge2[me_b], s.ge2r)
     spread(lambda peer: s.ge3.at[me_b], s.ge3.at[me_b], 4)
-    send_tokens(last)
 
     slot = lax.broadcasted_iota(jnp.int32, (T, L), 1)
     d_row, d_col = grid_of(slot)
@@ -711,6 +766,8 @@
             line = line + jnp.where(good, take(ordered[:, 0:128], ordered[:, 128:256], index), 0.0)
         bias_rows.append(total(line * s.rowmask[...]))
     start_sum(5, bias_rows)
+    for i in range(1, n // GB):
+        send_tokens(i)
 
     shares_done((s.gl1, s.gl1r), 8)
     s.gl2[...] = head_sum((s.gl1, s.gl1r)).reshape(B, z.rl // B, 128)
@@ -745,18 +802,20 @@
     at = lax.broadcasted_iota(jnp.int32, (128, 128), 0)
     to = lax.broadcasted_iota(jnp.int32, (128, 128), 1)
     turn = jnp.where(lax.bitwise_and(at, 7) * 16 + lax.shift_right_logical(at, 3) == to, 1.0, 0.0).astype(bf16)
+    whole = z.share // 16 * 16
     for src, dst in ((out_i, out), (tg_i, tg)):
-        rows = z.share // 16 * 16
-        for k in range(0, rows, 16):
-            dst[k : k + 16] = nn(turn, src[:, k : k + 16, :].reshape(128, z.D)).reshape(16, 8, z.D)
-        for k in range(rows, z.share):
-            dst[k] = src[:, k, :].astype(f32)
+        for i in range(0, src.shape[0], 8):
+            for k in range(0, whole, 16):
+                rows = src[i : i + 8, k : k + 16, :].reshape(128, z.D)
+                dst[k : k + 16, i : i + 8, :] = nn(turn, rows).reshape(16, 8, z.D)
+            for k in range(whole, z.share):
+                dst[k, i : i + 8, :] = src[i : i + 8, k, :].astype(f32)
 
     @pl.when(pl.program_id(0) == 0)
     def _():
         D, C, PH = z.D, z.C, z.D // z.H
-        up[...] = early[0:D, :]
-        down[...] = early[D : 2 * D, :].T
+        down[...] = early[0:D, :].T
+        up[...] = early[D : 2 * D, :]
         for half in range(D // 128):
             lanes = slice(half * 128, (half + 1) * 128)
             proj[:, lanes] = early[2 * D + half * PH : 2 * D + (half + 1) * PH, :]
@@ -819,9 +878,9 @@
         cotangent.transpose(1, 0, 2),
     )
 
-    steps = images // 8
-    block = pl.BlockSpec((8, z.share, width), lambda i: (i, 0, 0))
-    turned = pl.BlockSpec((z.share, 8, width), lambda i: (0, i, 0))
+    steps = 2
+    block = pl.BlockSpec((images // steps, z.share, width), lambda i: (i, 0, 0))
+    turned = pl.BlockSpec((z.share, images // steps, width), lambda i: (0, i, 0))
 
     def whole(*shape):
         return jax.ShapeDtypeStruct(shape, f32), pl.BlockSpec(shape, lambda i: (0,) * len(shape))
@@ -837,6 +896,7 @@
         out_shape=[big, big] + [a for a, _ in small],
         in_specs=[block, block, whole(z.re, 128)[1], whole(z.rl, 128)[1], whole(8, width)[1]],
         out_specs=[turned, turned] + [b for _, b in small],
+        compiler_params=pltpu.CompilerParams(vmem_limit_bytes=32 * 1024 * 1024),
     )(*outs)
     res = [res[0].transpose(1, 0, 2), res[1].transpose(1, 0, 2), *res[2:]]
     for k in (5, 6, 8, 9, 11, 12):

time: 106 us -> 102 us (0.962)
  Pallas kernels: 104 us -> 94.7 us
  local copies, waits for them, and re-layouts: 0 us -> 5.24 us
    pallas_call x1, Pallas kernels: 97.7 us -> 91.8 us  [on_device(): pl.pallas_call(functools.partial(block_kernel, z, tuple(scratch)), out_sh...]
    unnamed x0 -> x10, local copies, waits for them, and re-layouts: none -> 5.24 us
    pallas_call x1, Pallas kernels: 6.83 us -> 2.91 us  [on_device(): pl.pallas_call(functools.partial(finish_kernel, z), grid=(steps,), out_sh...]
where the time goes in v4:
time: 102 us; the launch traced here: 101 us
  Pallas kernels  94.7 us (93%)
  local copies, waits for them, and re-layouts  5.24 us (5%)
  between operations  1.47 us (1%)
    pallas_call x1, Pallas kernels, on_device(): pl.pallas_call(functools.partial(block_kernel, z, tuple(scratch)), out_sh...  91.8 us
    unnamed x10, local copies, waits for them, and re-layouts  5.24 us
    pallas_call x1, Pallas kernels, on_device(): pl.pallas_call(functools.partial(finish_kernel, z), grid=(steps,), out_sh...  2.91 us

profile of v4, /device:TPU:0, one launch (start us, length us, event | category | flops | bytes accessed | tf_op | source)
XLA Modules:
  0.0 101.4 jit_solution(13109549115052526543)
XLA Ops:
  1.3 91.8 %shard_map.246 = (bf16[48,49,256]{2,1,0:T(8,128)(2,1)}, bf16[48,49,256]{2,1,0:T(8,128)(2,1)}, f32[640,128]{1,0:T(8,128)}, f32[256,128]{1,0:T(8,128)}, f32[8,256]{1,0:T(8,128)}) custom-call(bf16[196,48,256]{2,1,0:T(8,128)(2,1)} %bitcast.17, s32[1]{0:T(128)S(6)} %copy.28.refs_1_, s32[1,196]{1,0:T(1,128)} %bitcast.19, f32[1,128,256]{2,1,0:T(8,128)} %refs_3_.1, ...), custom_call_target="tpu_custom_call" | custom-call | tf_op jit(solution)/shard_map/pallas_call | solution.py:859
  93.1 0.0 copy-start
  93.1 1.3 %copy-done = bf16[48,49,256]{2,1,0:T(8,128)(2,1)S(1)} copy-done((bf16[48,49,256]{2,1,0:T(8,128)(2,1)S(1)}, bf16[48,49,256]{2,1,0:T(8,128)(2,1)}, u32[]{:S(2)}) %copy-start) | copy-done | bytes 1204248
  94.4 0.0 copy-start.1
  94.4 1.3 %copy-done.1 = bf16[48,49,256]{2,1,0:T(8,128)(2,1)S(1)} copy-done((bf16[48,49,256]{2,1,0:T(8,128)(2,1)S(1)}, bf16[48,49,256]{2,1,0:T(8,128)(2,1)}, u32[]{:S(2)}) %copy-start.1) | copy-done | bytes 1204248
  95.8 0.0 copy-start.2
  95.8 1.0 copy-done.2
  96.7 0.0 copy-start.3
  96.7 0.9 copy-done.3
  97.6 0.0 copy-start.4
  97.6 0.7 copy-done.4
  98.3 2.9 %shard_map.247 = (f32[49,48,256]{2,1,0:T(8,128)}, f32[49,48,256]{2,1,0:T(8,128)}, f32[1,128,256]{2,1,0:T(8,128)}, f32[1,196]{1,0:T(1,128)}, f32[64,256]{1,0:T(8,...) custom-call(bf16[48,49,256]{2,1,0:T(8,128)(2,1)S(1)} %copy-done, ...), custom_call_target="tpu_custom_call" | custom-call | tf_op jit(solution)/shard_map/pallas_call | solution.py:893
Async XLA Ops:
  93.1 1.3 %copy-start = (bf16[48,49,256]{2,1,0:T(8,128)(2,1)S(1)}, bf16[48,49,256]{2,1,0:T(8,128)(2,1)}, u32[]{:S(2)}) copy-start(bf16[48,49,256]{2,1,0:T(8,128)(2,1)} %get-tuple-element.31.out_i) | copy-start | bytes 3612676
  94.4 1.3 %copy-start.1 = (bf16[48,49,256]{2,1,0:T(8,128)(2,1)S(1)}, bf16[48,49,256]{2,1,0:T(8,128)(2,1)}, u32[]{:S(2)}) copy-start(bf16[48,49,256]{2,1,0:T(8,128)(2,1)} %get-tuple-element.32.tg_i) | copy-start | bytes 3612676
  95.8 1.0 copy-start.2
  96.7 0.9 copy-start.3
  97.6 0.7 copy-start.4

commit v5 on v4

--- a/solution.py
+++ b/solution.py
@@ -568,16 +568,20 @@
         for j in range(1, H):
             to_head(s.ge1.at[head_peers[j], rows], s.ge1r.at[me_h, rows], 7, j).start()
 
-    def send_output(i):
-        to = out_o.at[pl.ds(me_h * n + i * G, G)]
-        for j in range(1, H):
-            to_head(s.osend.at[head_peers[j], pl.ds(i * G, G)], to, 5, j).start()
+    def send_output(low, high):
+        low, high = low * n // 12, high * n // 12
+        if high > low:
+            to = out_o.at[pl.ds(me_h * n + low, high - low)]
+            for j in range(1, H):
+                to_head(s.osend.at[head_peers[j], pl.ds(low, high - low)], to, 5, j).start()
 
     first, second = lax.fori_loop(0, n // G, back_leave, (zeros(F), zeros(F)))
     start_sum(3, [total(first), total(second)])
     output(0)
-    send_output(0)
+    send_output(0, 4)
     lax.fori_loop(0, n // G, down_gradient, 0)
+    for i in range(1, n // G):
+        output(i)
     early(0, [s.gdown[:, h * FH : (h + 1) * FH] for h in range(H)])
     sums = finish_sum(3, F)
 
@@ -607,8 +611,6 @@
     lax.fori_loop(0, n // G, up_gradient, 0)
     early(D, [s.gup[:, h * FH : (h + 1) * FH] for h in range(H)])
     send_early(D, 2 * D)
-    for i in range(1, n // G):
-        output(i)
     sums = finish_sum(4, D)
     c_out = local(s.osend.at[me_h], out_o.at[pl.ds(me_h * n, n)], 6)
     sum_shift_1 = sums[0]
@@ -661,8 +663,7 @@
     if z.re > filled:
         s.ge1[:, filled:, :] = jnp.zeros((H, z.re - filled, 128), bf16)
     send_early(2 * D, z.re)
-    for i in range(1, n // G):
-        send_output(i)
+    send_output(4, 12)
 
     GB = z.group_back
 
@@ -896,7 +897,7 @@
         out_shape=[big, big] + [a for a, _ in small],
         in_specs=[block, block, whole(z.re, 128)[1], whole(z.rl, 128)[1], whole(8, width)[1]],
         out_specs=[turned, turned] + [b for _, b in small],
-        compiler_params=pltpu.CompilerParams(vmem_limit_bytes=32 * 1024 * 1024),
+        compiler_params=pltpu.CompilerParams(vmem_limit_bytes=127 * 512 * 1024),
     )(*outs)
     res = [res[0].transpose(1, 0, 2), res[1].transpose(1, 0, 2), *res[2:]]
     for k in (5, 6, 8, 9, 11, 12):

time: 102 us -> 97.8 us (0.959)
  local copies, waits for them, and re-layouts: 5.24 us -> 0 us
  Pallas kernels: 94.7 us -> 96.1 us
    unnamed x10 -> x0, local copies, waits for them, and re-layouts: 5.24 us -> none
    pallas_call x1, Pallas kernels: 2.91 us -> 4.38 us  [on_device(): pl.pallas_call(functools.partial(finish_kernel, z), grid=(steps,), out_sh...]
where the time goes in v5:
time: 97.8 us; the launch traced here: 97.6 us
  Pallas kernels  96.1 us (98%)
  between operations  1.46 us (1%)
    pallas_call x1, Pallas kernels, on_device(): pl.pallas_call(functools.partial(block_kernel, z, tuple(scratch)), out_sh...  91.7 us
    pallas_call x1, Pallas kernels, on_device(): pl.pallas_call(functools.partial(finish_kernel, z), grid=(steps,), out_sh...  4.38 us

profile of v5, /device:TPU:0, one launch (start us, length us, event | category | flops | bytes accessed | tf_op | source)
XLA Modules:
  0.0 97.6 jit_solution(10849770893774493985)
XLA Ops:
  1.3 91.7 %shard_map.246 = (bf16[48,49,256]{2,1,0:T(8,128)(2,1)}, bf16[48,49,256]{2,1,0:T(8,128)(2,1)}, f32[640,128]{1,0:T(8,128)}, f32[256,128]{1,0:T(8,128)}, f32[8,256]{1,0:T(8,128)}) custom-call(bf16[196,48,256]{2,1,0:T(8,128)(2,1)} %bitcast.17, s32[1]{0:T(128)S(6)} %copy.28.refs_1_, s32[1,196]{1,0:T(1,128)} %bitcast.19, f32[1,128,256]{2,1,0:T(8,128)} %refs_3_.1, ...), custom_call_target="tpu_custom_call" | custom-call | tf_op jit(solution)/shard_map/pallas_call | solution.py:860
  93.0 4.4 %shard_map.247 = (f32[49,48,256]{2,1,0:T(8,128)}, f32[49,48,256]{2,1,0:T(8,128)}, f32[1,128,256]{2,1,0:T(8,128)}, f32[1,196]{1,0:T(1,128)}, f32[64,256]{1,0:T(8,...) custom-call(bf16[48,49,256]{2,1,0:T(8,128)(2,1)} %get-tuple-element., ...), custom_call_target="tpu_custom_call" | custom-call | tf_op jit(solution)/shard_map/pallas_call | solution.py:894

commit v6 on v5

--- a/solution.py
+++ b/solution.py
@@ -236,6 +236,16 @@
     c_down.wait()
     s.downg[me_h, down_rows] = s.gdown[down_rows, 0:D].astype(bf16)
 
+    s.cnt[me_b] = jnp.full((1, 128), count[0]).astype(f32)
+    pl.semaphore_wait(barrier, H - 1 + B - 1)
+
+    shared = (s.qkvg.at[me_h], s.smallg.at[me_h], s.upcat.at[up_rows, own], s.downg.at[me_h, down_rows])
+    for k in (1, 0, 2, 3):
+        for j in range(1, H):
+            to_head(shared[k], shared[k], k, j).start()
+    greet(s.ready)
+
+    around(B, lambda j: to_batch(s.cnt.at[me_b], s.cnt.at[me_b], 0, lax.rem(me_b + j, B)).start())
     row_at = lax.broadcasted_iota(jnp.int32, (L, L), 0)
     lane_at = lax.broadcasted_iota(jnp.int32, (L, L), 1)
     s.rowmask[...] = jnp.where(row_at < length, 1.0, 0.0)[0:T]
@@ -332,15 +342,6 @@
             at = q * share + share // 16 * 16
             s.u[i, at : at + 1, :] = rest[i : i + 1] * valid_of(i)
 
-    s.cnt[me_b] = jnp.full((1, 128), count[0]).astype(f32)
-    pl.semaphore_wait(barrier, H - 1 + B - 1)
-
-    shared = (s.qkvg.at[me_h], s.smallg.at[me_h], s.upcat.at[up_rows, own], s.downg.at[me_h, down_rows])
-    for k in (1, 0, 2, 3):
-        for j in range(1, H):
-            to_head(shared[k], shared[k], k, j).start()
-    greet(s.ready)
-
     cuts = (0, blocks * 6 // 10, blocks)
 
     def send_cotangent(piece):
@@ -349,7 +350,6 @@
             to_head(s.xt.at[pl.ds(head_peers[j] * blocks + low, high - low)],
                     s.ct.at[pl.ds(me_h * blocks + low, high - low)], 4, j).start()
 
-    around(B, lambda j: to_batch(s.cnt.at[me_b], s.cnt.at[me_b], 0, lax.rem(me_b + j, B)).start())
     send_cotangent(0)
 
     some = pl.ds(0, H - 1)
@@ -515,7 +515,6 @@
         shaped = group(s.hid, i) * a_2 + b_2
         gate = sigmoid(shaped)
         active = shaped * gate
-        put(s.slope, i, gate + active * (1.0 - gate))
         low = active.astype(bf16)
         put(s.act2, i, low)
         outgoing = nn(low, down)
@@ -527,6 +526,14 @@
 
     sums = lax.fori_loop(0, n // G, leave, (zeros(D), zeros(D), zeros(D), zeros(D)))
     start_sum(2, [total(v) for v in sums])
+
+    def slope(i, carry):
+        shaped = group(s.hid, i) * a_2 + b_2
+        gate = sigmoid(shaped)
+        put(s.slope, i, gate + shaped * gate * (1.0 - gate))
+        return carry
+
+    lax.fori_loop(0, n // G, slope, 0)
     sums = finish_sum(2, D)
     mean_3, inverse_3 = moments(sums[0], sums[1], seen_row)
     a_3 = gain_3[...] * inverse_3
@@ -767,9 +774,9 @@
             line = line + jnp.where(good, take(ordered[:, 0:128], ordered[:, 128:256], index), 0.0)
         bias_rows.append(total(line * s.rowmask[...]))
     start_sum(5, bias_rows)
+
     for i in range(1, n // GB):
         send_tokens(i)
-
     shares_done((s.gl1, s.gl1r), 8)
     s.gl2[...] = head_sum((s.gl1, s.gl1r)).reshape(B, z.rl // B, 128)
     spread(lambda peer: s.gl2.at[peer], s.gl2r.at[me_b], 5)

time: 97.8 us -> 93.5 us (0.956)
  Pallas kernels: 96.1 us -> 91.9 us
    pallas_call x1, Pallas kernels: 91.7 us -> 87.5 us  [on_device(): pl.pallas_call(functools.partial(block_kernel, z, tuple(scratch)), out_sh...]
where the time goes in v6:
time: 93.5 us; the launch traced here: 93.4 us
  Pallas kernels  91.9 us (98%)
  between operations  1.46 us (2%)
    pallas_call x1, Pallas kernels, on_device(): pl.pallas_call(functools.partial(block_kernel, z, tuple(scratch)), out_sh...  87.5 us
    pallas_call x1, Pallas kernels, on_device(): pl.pallas_call(functools.partial(finish_kernel, z), grid=(steps,), out_sh...  4.38 us

profile of v6, /device:TPU:0, one launch (start us, length us, event | category | flops | bytes accessed | tf_op | source)
XLA Modules:
  0.0 93.4 jit_solution(1762857127940292462)
XLA Ops:
  1.3 87.5 %shard_map.246 = (bf16[48,49,256]{2,1,0:T(8,128)(2,1)}, bf16[48,49,256]{2,1,0:T(8,128)(2,1)}, f32[640,128]{1,0:T(8,128)}, f32[256,128]{1,0:T(8,128)}, f32[8,256]{1,0:T(8,128)}) custom-call(bf16[196,48,256]{2,1,0:T(8,128)(2,1)} %bitcast.17, s32[1]{0:T(128)S(6)} %copy.28.refs_1_, s32[1,196]{1,0:T(1,128)} %bitcast.19, f32[1,128,256]{2,1,0:T(8,128)} %refs_3_.1, ...), custom_call_target="tpu_custom_call" | custom-call | tf_op jit(solution)/shard_map/pallas_call | solution.py:867
  88.8 4.4 %shard_map.247 = (f32[49,48,256]{2,1,0:T(8,128)}, f32[49,48,256]{2,1,0:T(8,128)}, f32[1,128,256]{2,1,0:T(8,128)}, f32[1,196]{1,0:T(1,128)}, f32[64,256]{1,0:T(8,...) custom-call(bf16[48,49,256]{2,1,0:T(8,128)(2,1)} %get-tuple-element., ...), custom_call_target="tpu_custom_call" | custom-call | tf_op jit(solution)/shard_map/pallas_call | solution.py:901

commit v7 on v6

--- a/solution.py
+++ b/solution.py
@@ -141,6 +141,8 @@
         "gl2": vmem((B, z.rl // B, 128), f32),
         "gl2r": vmem((B, z.rl // B, 128), f32),
         "gl3": vmem((B, z.rl // B, 128), f32),
+        **{"vector%d" % k: vmem((1, size), kind) for k, (size, kind) in enumerate(z.vectors)},
+        "vec": dma((len(z.vectors),)),
         "loc": dma((8,)),
         "hs": dma((9,)),
         "hr": dma((9,)),
@@ -190,6 +192,13 @@
         else:
             lax.fori_loop(1, size, lambda j, c: (step(j), c)[1], 0)
 
+    vectors = (place, table, gain_1, shift_1, gain_2, shift_2, gain_3, shift_3)
+    kept = [getattr(s, "vector%d" % k) for k in range(len(vectors))]
+    fetched = [pltpu.make_async_copy(src, dst, s.vec.at[k]) for k, (src, dst) in enumerate(zip(vectors, kept))]
+    for copy in fetched:
+        copy.start()
+    place, table, gain_1, shift_1, gain_2, shift_2, gain_3, shift_3 = kept
+
     FH = F // H
     PH = D // H
     own = pl.ds(pl.multiple_of(me_h * FH, FH), FH)
@@ -214,16 +223,17 @@
         return {"head": other, "batch": lax.rem(me_b + b, B)}
 
     barrier = pltpu.get_barrier_semaphore()
-    for j in range(1, H):
-        pl.semaphore_signal(barrier, inc=1, device_id={"head": head_peers[j]}, device_id_type=MESH)
-
     def greet(semaphore):
         around(B, lambda j: pl.semaphore_signal(
             semaphore, inc=1, device_id={"batch": lax.rem(me_b + j, B)}, device_id_type=MESH))
 
     greet(barrier)
+    for j in range(1, H):
+        pl.semaphore_signal(barrier, inc=1, device_id={"head": head_peers[j]}, device_id_type=MESH)
     targets = [at_offset(*pair) for pair in everyone()] if z.direct else []
 
+    for copy in fetched:
+        copy.wait()
     s.smallg[me_h] = jnp.concatenate(
         [gain_2[...], shift_2[...], table[:, 0:128], jnp.concatenate(
             [table[:, 128:length], jnp.zeros((1, 256 - length), f32)], axis=1)], axis=0)
@@ -860,6 +870,8 @@
         return first, None if z.direct else getattr(s, "part%d" % (k % 2)).at[:, 0 : first.shape[1]]
 
     z.bufs = bufs
+    z.vectors = [(length, jnp.int32), (length, f32), (width, f32), (width, f32)]
+    z.vectors += [(z.F // H, f32)] * 2 + [(width, f32)] * 2
     scratch = layout(z)
     hbm = pl.BlockSpec(memory_space=pl.ANY)
     vmem = pl.BlockSpec(memory_space=pltpu.VMEM)
@@ -873,7 +885,7 @@
             jax.ShapeDtypeStruct((z.rl, 128), f32),
             jax.ShapeDtypeStruct((8, width), f32),
         ),
-        in_specs=[hbm, smem, vmem, hbm, vmem, hbm, vmem, vmem, hbm, vmem, vmem, hbm, vmem, vmem, hbm],
+        in_specs=[hbm, smem] + [hbm] * 13,
         out_specs=(hbm, hbm, vmem, vmem, vmem),
         scratch_shapes=list(scratch.values()),
         compiler_params=pltpu.CompilerParams(

time: 93.5 us -> 93.1 us (level)
  no operation moved by 1% of the time
where the time goes in v7:
time: 93.1 us; the launch traced here: 92.9 us
  Pallas kernels  91.5 us (98%)
  between operations  1.46 us (2%)
    pallas_call x1, Pallas kernels, on_device(): pl.pallas_call(functools.partial(block_kernel, z, tuple(scratch)), out_sh...  87.1 us
    pallas_call x1, Pallas kernels, on_device(): pl.pallas_call(functools.partial(finish_kernel, z), grid=(steps,), out_sh...  4.38 us

profile of v7, /device:TPU:0, one launch (start us, length us, event | category | flops | bytes accessed | tf_op | source)
XLA Modules:
  0.0 92.9 jit_solution(7414775908183292009)
XLA Ops:
  1.3 87.1 %shard_map.246 = (bf16[48,49,256]{2,1,0:T(8,128)(2,1)}, bf16[48,49,256]{2,1,0:T(8,128)(2,1)}, f32[640,128]{1,0:T(8,128)}, f32[256,128]{1,0:T(8,128)}, f32[8,256]{1,0:T(8,128)}) custom-call(bf16[196,48,256]{2,1,0:T(8,128)(2,1)} %bitcast.17, s32[1]{0:T(128)S(6)} %copy.28.refs_1_, s32[1,196]{1,0:T(1,128)} %bitcast.19, f32[1,128,256]{2,1,0:T(8,128)} %refs_3_.1, ...), custom_call_target="tpu_custom_call" | custom-call | tf_op jit(solution)/shard_map/pallas_call | solution.py:879
  88.4 4.4 %shard_map.247 = (f32[49,48,256]{2,1,0:T(8,128)}, f32[49,48,256]{2,1,0:T(8,128)}, f32[1,128,256]{2,1,0:T(8,128)}, f32[1,196]{1,0:T(1,128)}, f32[64,256]{1,0:T(8,...) custom-call(bf16[48,49,256]{2,1,0:T(8,128)(2,1)} %get-tuple-element., ...), custom_call_target="tpu_custom_call" | custom-call | tf_op jit(solution)/shard_map/pallas_call | solution.py:913

commit v8 on v7

--- a/solution.py
+++ b/solution.py
@@ -457,6 +457,7 @@
 
     first, second = lax.fori_loop(0, n // z.group, attend, (zeros(D), zeros(D)))
     pl.semaphore_wait(s.ready, B - 1)
+    start_sum(0, [total(first), total(second)])
     some_rows = pl.ds(0, D // 2)
     done(to_head(s.upcat.at[some_rows, pl.ds(0, FH * (H - 1))], s.upcat.at[some_rows, pl.ds(0, FH * (H - 1))], 2, 1))
     down_some = s.downg.at[some, pl.ds(0, FH // 2)]
@@ -464,7 +465,6 @@
     halves = (s.upcat.at[up_rows, :], s.downg.at[:, down_rows])
     for k in range(2):
         to_batch(halves[k], halves[k], k + 1, sibling).start()
-    start_sum(0, [total(first), total(second)])
     send_cotangent(1)
     for k in range(2):
         to_batch(halves[k], halves[k], k + 1, sibling).wait()

time: 93.1 us -> 93.1 us (level)
  no operation moved by 1% of the time
where the time goes in v8:
time: 93.1 us; the launch traced here: 92.9 us
  Pallas kernels  91.4 us (98%)
  between operations  1.46 us (2%)
    pallas_call x1, Pallas kernels, on_device(): pl.pallas_call(functools.partial(block_kernel, z, tuple(scratch)), out_sh...  87.1 us
    pallas_call x1, Pallas kernels, on_device(): pl.pallas_call(functools.partial(finish_kernel, z), grid=(steps,), out_sh...  4.38 us

profile of v8, /device:TPU:0, one launch (start us, length us, event | category | flops | bytes accessed | tf_op | source)
XLA Modules:
  0.0 92.9 jit_solution(15079899495958793036)
XLA Ops:
  1.3 87.1 %shard_map.246 = (bf16[48,49,256]{2,1,0:T(8,128)(2,1)}, bf16[48,49,256]{2,1,0:T(8,128)(2,1)}, f32[640,128]{1,0:T(8,128)}, f32[256,128]{1,0:T(8,128)}, f32[8,256]{1,0:T(8,128)}) custom-call(bf16[196,48,256]{2,1,0:T(8,128)(2,1)} %bitcast.17, s32[1]{0:T(128)S(6)} %copy.28.refs_1_, s32[1,196]{1,0:T(1,128)} %bitcast.19, f32[1,128,256]{2,1,0:T(8,128)} %refs_3_.1, ...), custom_call_target="tpu_custom_call" | custom-call | tf_op jit(solution)/shard_map/pallas_call | solution.py:879
  88.4 4.4 %shard_map.247 = (f32[49,48,256]{2,1,0:T(8,128)}, f32[49,48,256]{2,1,0:T(8,128)}, f32[1,128,256]{2,1,0:T(8,128)}, f32[1,196]{1,0:T(1,128)}, f32[64,256]{1,0:T(8,...) custom-call(bf16[48,49,256]{2,1,0:T(8,128)(2,1)} %get-tuple-element., ...), custom_call_target="tpu_custom_call" | custom-call | tf_op jit(solution)/shard_map/pallas_call | solution.py:913
